TPU v7x, 32 devices: a whole 2x2x4 slice. The times are simulated.
32 devices in a mesh: dp: 16 (over z, y, x), tensor: 2 (over core).
Axes of the slice: x: 2, y: 2, z: 4, core: 2. Of those that a mesh axis runs over, the one named last changes fastest.
Arguments:
- tokens: bfloat16 [16, 1024, 768], P('dp'), may hold values from -6 to 6
- gain_attn: float32 [768], replicated, may hold values from 0.5 to 1.5
- query_key_value_weight: bfloat16 [3, 768, 768], P(None, None, 'tensor'), may hold values from -0.21875 to 0.21875
- attn_out_weight: bfloat16 [768, 768], P('tensor'), may hold values from -0.875 to 0.875
- position_bias_matrix: float32 [32, 12], P(None, 'tensor'), may hold values from -4 to 4
- gain_expert: float32 [768], replicated, may hold values from 0.5 to 1.5
- router: float32 [768, 4], replicated, may hold values from -0.21875 to 0.21875
- expert_in: bfloat16 [4, 768, 3072], P(None, None, 'tensor'), may hold values from -0.21875 to 0.21875
- expert_out: bfloat16 [4, 3072, 768], P(None, 'tensor'), may hold values from -0.4375 to 0.4375
- segments: int32 [16, 1024], P('dp'), may hold values from 0 to 3, never falling along the last dimension, each value on 1 to 512 neighbouring positions
- routes: int32 [16, 1024], P('dp'), may hold values from 0 to 3, as said below
- slots: int32 [16, 1024], P('dp'), may hold values from 0 to 319, as said below
- cotangent: bfloat16 [16, 1024, 768], P('dp'), may hold values from -6 to 6
Outputs:
- output: bfloat16 [16, 1024, 768], P('dp')
- grad_tokens: float32 [16, 1024, 768], P('dp')
- grad_gain_attn: float32 [768], P('dp')
- projection_weight_gradient: float32 [3, 768, 768], P(None, 'dp', 'tensor')
- grad_attn_out: float32 [768, 768], P('tensor', 'dp')
- grad_bias_table: float32 [32, 12], P(None, 'tensor')
- grad_gain_expert: float32 [768], P('dp')
- grad_router: float32 [768, 4], P('dp')
- grad_expert_in: float32 [4, 768, 3072], P(None, 'dp', 'tensor')
- grad_expert_out: float32 [4, 3072, 768], P(None, 'tensor', 'dp')
Inputs may be any that keep to these rules, and one draw needn't show every extreme that they name: `routes`: within each aligned block of 1 sequence no two tokens have both the same route and the same slot, so an expert holds at most 320 tokens of a block; in every block some expert holds exactly 320. `slots`: paired with routes as stated there.
All inputs are finite; a program needn't handle non-finite values.
Results may differ from a plain program's by a relative error of at most 0.02.
Values may be sent and summed in bfloat16 or wider, within the bound.
A program may use at most 320 MiB of HBM per device.

v0:
```python
import jax
import jax.numpy as jnp
from jax import lax
from jax.sharding import PartitionSpec as P

HEAD_DIM = 64
CAP = 320


EPS = 1e-06
NEG = -1e30
HIGH = lax.Precision.HIGHEST


def relative_bucket_index(length):
    places = jnp.arange(length, dtype=jnp.int32)
    offset = places[None, :] - places[:, None]
    distance = jnp.abs(offset)
    coarse = jnp.full_like(distance, 8)
    for limit in (12, 16, 23, 32, 46, 64, 91):
        coarse = coarse + (distance >= limit).astype(jnp.int32)
    bucket = jnp.where(distance < 8, distance, coarse)
    return bucket + 16 * (offset > 0).astype(jnp.int32)


def bucket_blocks(bucket):
    length = bucket.shape[0]
    rows = min(128, length)
    return bucket.reshape(length // rows, rows, length)


def bucket_onehot(bucket_rows, count):
    labels = jnp.arange(count, dtype=jnp.int32)
    return (bucket_rows[..., None] == labels).astype(jnp.float32)


def expand_bias(table, bucket):
    blocked = bucket_blocks(bucket)
    count = table.shape[0]

    def expand_one_rows(bucket_rows):
        return jnp.einsum(
            "ijb,bh->hij",
            bucket_onehot(bucket_rows, count),
            table,
            precision=HIGH,
            preferred_element_type=jnp.float32,
        )

    pieces = lax.map(expand_one_rows, blocked)
    length = bucket.shape[0]
    return jnp.transpose(pieces, (1, 0, 2, 3)).reshape(table.shape[1], length, length)


def table_grad_of(score_sum, bucket, count):
    blocked = bucket_blocks(bucket)
    heads = score_sum.shape[0]
    score_rows = jnp.transpose(
        score_sum.reshape(heads, blocked.shape[0], blocked.shape[1], blocked.shape[2]), (1, 0, 2, 3)
    )

    def table_one_rows(item):
        bucket_rows, score_piece = item
        return jnp.einsum(
            "hij,ijb->bh",
            score_piece,
            bucket_onehot(bucket_rows, count),
            precision=HIGH,
            preferred_element_type=jnp.float32,
        )

    return jnp.sum(lax.map(table_one_rows, (blocked, score_rows)), axis=0)


def row_norm(values, gain):
    inverse = lax.rsqrt(jnp.mean(values * values, axis=-1, keepdims=True) + EPS)
    return (values * inverse * gain, inverse)


def norm_back(grad_out, values, inverse, gain):
    scaled = grad_out * gain
    grad_gain = jnp.sum(grad_out * values * inverse, axis=0)
    grad_in = inverse * scaled - values * inverse**3 * jnp.mean(
        scaled * values, axis=-1, keepdims=True
    )
    return (grad_in, grad_gain)


def scores_of(query, keys, bias, segment, scale):
    raw = jnp.einsum("ihd,jhd->hij", query, keys, preferred_element_type=jnp.float32) * scale
    same = segment[:, None] == segment[None, :]
    return jnp.where(same[None], raw + bias, NEG)


def body(
    tokens,
    gain_attn,
    query_key_value_weight,
    attn_out_weight,
    position_bias_matrix,
    gain_expert,
    router,
    expert_in,
    expert_out,
    segments,
    routes,
    slots,
    cotangent,
):
    seqs, length, width = tokens.shape
    local_heads = position_bias_matrix.shape[1]
    head_size = HEAD_DIM
    scale = head_size ** (-0.5)
    count = seqs * length
    experts = expert_in.shape[0]
    capacity = CAP
    inputs = tokens.astype(jnp.float32).reshape(count, width)
    normed_a, inverse_a = row_norm(inputs, gain_attn)
    act_a = normed_a.astype(jnp.bfloat16)
    projected = jnp.einsum(
        "td,cde->cte", act_a, query_key_value_weight, preferred_element_type=jnp.float32
    ).astype(jnp.bfloat16)
    shaped = projected.reshape(3, seqs, length, local_heads, head_size)
    bucket = relative_bucket_index(length)
    bias = expand_bias(position_bias_matrix, bucket)

    def attend(item):
        query, keys, values, segment = item
        scores = scores_of(query, keys, bias, segment, scale)
        peak = jnp.max(scores, axis=-1, keepdims=True)
        expo = jnp.exp(scores - peak)
        total = jnp.sum(expo, axis=-1, keepdims=True)
        probs = (expo / total).astype(jnp.bfloat16)
        mixed = jnp.einsum("hij,jhd->ihd", probs, values, preferred_element_type=jnp.float32)
        return (
            mixed.astype(jnp.bfloat16).reshape(length, local_heads * head_size),
            (peak + jnp.log(total))[..., 0],
        )

    attended, logsum = lax.map(attend, (shaped[0], shaped[1], shaped[2], segments))
    flat_att = attended.reshape(count, local_heads * head_size)
    attention_partial_output = jnp.dot(
        flat_att, attn_out_weight, preferred_element_type=jnp.float32
    ).astype(jnp.bfloat16)
    attn_total = lax.psum(attention_partial_output, "tensor").astype(jnp.float32)
    hidden_res = inputs + attn_total
    expert_normed_input, inverse_e = row_norm(hidden_res, gain_expert)
    logits = jnp.dot(
        expert_normed_input, router, precision=HIGH, preferred_element_type=jnp.float32
    )
    chance = jax.nn.softmax(logits, axis=-1)
    route_flat = routes.reshape(count)
    onehot = (route_flat[:, None] == jnp.arange(experts, dtype=jnp.int32)[None, :]).astype(
        jnp.float32
    )
    gate = jnp.sum(chance * onehot, axis=-1)
    place = route_flat * capacity + slots.reshape(count)
    act_e = expert_normed_input.astype(jnp.bfloat16)
    dispatched = (
        jnp.zeros((experts * capacity, width), jnp.bfloat16)
        .at[place]
        .set(act_e)
        .reshape(experts, capacity, width)
    )
    inner = jnp.einsum("ecd,edf->ecf", dispatched, expert_in, preferred_element_type=jnp.float32)
    activated = jax.nn.gelu(inner).astype(jnp.bfloat16)
    returned = jnp.einsum("ecf,efd->ecd", activated, expert_out, preferred_element_type=jnp.float32)
    returned = returned.astype(jnp.bfloat16).reshape(experts * capacity, width)
    expert_total = lax.psum(returned[place], "tensor").astype(jnp.float32)
    result = hidden_res + expert_total * gate[:, None]
    output = result.astype(jnp.bfloat16).reshape(seqs, length, width)
    upstream = cotangent.astype(jnp.float32).reshape(count, width)
    grad_gate = jnp.sum(upstream * expert_total, axis=-1)
    scaled_up = (upstream * gate[:, None]).astype(jnp.bfloat16)
    slot_grad = (
        jnp.zeros((experts * capacity, width), jnp.bfloat16)
        .at[place]
        .set(scaled_up)
        .reshape(experts, capacity, width)
    )
    grad_expert_out = jnp.einsum(
        "ecf,ecd->efd", activated, slot_grad, preferred_element_type=jnp.float32
    )
    grad_act = jnp.einsum("ecd,efd->ecf", slot_grad, expert_out, preferred_element_type=jnp.float32)
    unused, gelu_pull = jax.vjp(jax.nn.gelu, inner)
    grad_inner = gelu_pull(grad_act)[0].astype(jnp.bfloat16)
    grad_expert_in = jnp.einsum(
        "ecd,ecf->edf", dispatched, grad_inner, preferred_element_type=jnp.float32
    )
    grad_disp = jnp.einsum(
        "ecf,edf->ecd", grad_inner, expert_in, preferred_element_type=jnp.float32
    ).reshape(experts * capacity, width)
    back_expert = lax.psum(grad_disp[place].astype(jnp.bfloat16), "tensor").astype(jnp.float32)
    grad_logits = (grad_gate * gate)[:, None] * (onehot - chance)
    grad_router = jnp.dot(
        expert_normed_input.T, grad_logits, precision=HIGH, preferred_element_type=jnp.float32
    )
    grad_normed_e = back_expert + jnp.dot(
        grad_logits, router.T, precision=HIGH, preferred_element_type=jnp.float32
    )
    grad_hidden_part, grad_gain_expert = norm_back(
        grad_normed_e, hidden_res, inverse_e, gain_expert
    )
    grad_hidden = upstream + grad_hidden_part
    grad_hidden_low = grad_hidden.astype(jnp.bfloat16)
    grad_attn_out = jnp.dot(flat_att.T, grad_hidden_low, preferred_element_type=jnp.float32)
    grad_attended = jnp.dot(
        grad_hidden_low, attn_out_weight.T, preferred_element_type=jnp.float32
    ).astype(jnp.bfloat16)
    grad_attended = grad_attended.reshape(seqs, length, local_heads, head_size)

    def attend_back(carry, item):
        query, keys, values, segment, grad_mixed, lse = item
        scores = scores_of(query, keys, bias, segment, scale)
        probs = jnp.exp(scores - lse[..., None])
        probs_low = probs.astype(jnp.bfloat16)
        grad_probs = jnp.einsum(
            "ihd,jhd->hij", grad_mixed, values, preferred_element_type=jnp.float32
        )
        grad_values = jnp.einsum(
            "hij,ihd->jhd", probs_low, grad_mixed, preferred_element_type=jnp.float32
        )
        inner_sum = jnp.sum(grad_probs * probs, axis=-1, keepdims=True)
        grad_scores = probs * (grad_probs - inner_sum)
        grad_low = grad_scores.astype(jnp.bfloat16)
        grad_query = (
            jnp.einsum("hij,jhd->ihd", grad_low, keys, preferred_element_type=jnp.float32) * scale
        )
        grad_keys = (
            jnp.einsum("hij,ihd->jhd", grad_low, query, preferred_element_type=jnp.float32) * scale
        )
        stacked = jnp.stack([grad_query, grad_keys, grad_values]).astype(jnp.bfloat16)
        return (carry + grad_scores, stacked.reshape(3, length, local_heads * head_size))

    score_init = jnp.zeros((local_heads, length, length), jnp.float32)
    score_sum, projection_gradient_parts = lax.scan(
        attend_back, score_init, (shaped[0], shaped[1], shaped[2], segments, grad_attended, logsum)
    )
    sequence_activations = act_a.reshape(seqs, length, width)
    projection_weight_gradient = jnp.einsum(
        "kip,kniz->npz",
        sequence_activations,
        projection_gradient_parts,
        preferred_element_type=jnp.float32,
    )
    grad_act_a = jnp.einsum(
        "jqak,qvk->jav",
        projection_gradient_parts,
        query_key_value_weight,
        preferred_element_type=jnp.float32,
    )
    grad_table = table_grad_of(score_sum, bucket, position_bias_matrix.shape[0])
    back_attn = lax.psum(grad_act_a.reshape(count, width).astype(jnp.bfloat16), "tensor").astype(
        jnp.float32
    )
    grad_in_part, grad_gain_attn = norm_back(back_attn, inputs, inverse_a, gain_attn)
    grad_tokens = (grad_hidden + grad_in_part).reshape(seqs, length, width)
    table_total = lax.psum(grad_table, "dp")
    (
        summed_qkv,
        summed_attn_out,
        summed_in,
        summed_out,
        summed_router,
        summed_gain_a,
        summed_gain_e,
    ) = (
        lax.psum_scatter(projection_weight_gradient, "dp", scatter_dimension=1, tiled=True),
        lax.psum_scatter(grad_attn_out, "dp", scatter_dimension=1, tiled=True),
        lax.psum_scatter(grad_expert_in, "dp", scatter_dimension=1, tiled=True),
        lax.psum_scatter(grad_expert_out, "dp", scatter_dimension=2, tiled=True),
        lax.psum_scatter(grad_router, "dp", scatter_dimension=0, tiled=True),
        lax.psum_scatter(grad_gain_attn, "dp", scatter_dimension=0, tiled=True),
        lax.psum_scatter(grad_gain_expert, "dp", scatter_dimension=0, tiled=True),
    )
    return (
        output,
        grad_tokens,
        summed_gain_a,
        summed_qkv,
        summed_attn_out,
        table_total,
        summed_gain_e,
        summed_router,
        summed_in,
        summed_out,
    )


def solution(mesh):
    in_specs = (
        P("dp", None, None),
        P(),
        P(None, None, "tensor"),
        P("tensor", None),
        P(None, "tensor"),
        P(),
        P(),
        P(None, None, "tensor"),
        P(None, "tensor", None),
        P("dp", None),
        P("dp", None),
        P("dp", None),
        P("dp", None, None),
    )
    out_specs = (
        P("dp", None, None),
        P("dp", None, None),
        P("dp"),
        P(None, "dp", "tensor"),
        P("tensor", "dp"),
        P(None, "tensor"),
        P("dp"),
        P("dp", None),
        P(None, "dp", "tensor"),
        P(None, "tensor", "dp"),
    )
    return jax.shard_map(body, mesh=mesh, in_specs=in_specs, out_specs=out_specs, check_vma=False)
```

profile of v0, /device:TPU:0, one launch (start us, length us, event | category | flops | bytes accessed | tf_op | source)
XLA Modules:
  0.0 1423.5 jit_solution(14299388513771517847)
XLA Ops:
  7.3 1.9 fusion.51
  9.8 3.6 convert_bitcast_fusion.1
  14.5 5.8 fusion.32
  20.3 61.6 %while.4 = (s32[]{:T(128)}, f32[8,6,128,1024]{3,1,2,0:T(8,128)}, s32[8,128,1024]{2,1,0:T(8,128)}, f32[32,6]{0,1:T(8,128)S(1)}, s32[]{:T(128)}) while((s32[]{:T(128)}, f32[8,6,128,1024]{3,1,2,0:T(8,128)}, s32[8,128,1024]{2,1,0:T(8,128)}, f32[32,6]{0,1:T(8,128)S(1)}, s32[]{:T(128)}) %tuple.80), condition=%wide.region_2.3_spmd, body=%wide.region_1.2_spmd.sunk | while | flops 306184192 | bytes 5768513 | solution.py:50
  21.4 6.6 bitcast_dynamic-update-slice_fusion.2
  29.1 6.6 bitcast_dynamic-update-slice_fusion.2
  36.8 6.6 bitcast_dynamic-update-slice_fusion.2
  44.5 6.6 bitcast_dynamic-update-slice_fusion.2
  52.3 6.6 bitcast_dynamic-update-slice_fusion.2
  59.9 6.6 bitcast_dynamic-update-slice_fusion.2
  67.6 6.6 bitcast_dynamic-update-slice_fusion.2
  75.4 6.6 bitcast_dynamic-update-slice_fusion.2
  82.0 26.5 %copy.40 = f32[6,8,128,1024]{3,2,1,0:T(8,128)} copy(f32[6,8,128,1024]{3,0,2,1:T(8,128)} %bitcast.182) | data formatting | bytes 50331648 | tf_op jit(solution)/shard_map/transpose | solution.py:52
  110.1 15.9 %fusion.114 = (f32[6,1024]{1,0:T(8,128)S(1)}, f32[6,1024,1024]{2,1,0:T(8,128)}) fusion(f32[6,8,128,1024]{3,2,1,0:T(8,128)} %copy.40, bf16[1024,6,64]{0,2,1:T(8,128)(2,1)S(1)} %bitcast.191, bf16[1024,6,64]{0,2,1:T(8,128)(2,1)S(1)} %bitcast.193, pred[1024,1024]{1,0:T(8,128)(4,1)} %broadcast_compare_fusion), kind=kOutput, calls=%fused_computation.155 | convolution fusion | flops 830466048 | bytes 52977664 | tf_op jit(solution)/shard_map/while/body/eval_jaxpr/ihd,jhd->hij/dot_general | solution.py:90
  126.0 11.4 fusion.15
  137.5 10.4 fusion.97
  148.9 2.2 convolution_convert_fusion.1
  151.1 23.2 %all-reduce.10.cloned.1.call-done = bf16[1024,768]{1,0:T(8,128)(2,1)} async-done(((bf16[1024,768]{1,0:T(8,128)(2,1)}), bf16[1024,768]{1,0:T(8,128)(2,1)}) %all-reduce.10.cloned.1.call-update) | async-done | bytes 1572880 | tf_op jit(solution)/shard_map/psum | solution.py:145
  174.3 2.1 multiply_reduce_fusion.3
  176.5 3.3 fusion.115
  179.8 7.6 scatter_custom_fusion.1
  187.4 10.6 fusion.116
  198.0 8.2 scatter_custom_fusion
  206.2 13.8 fusion.27
  220.0 9.5 fusion.117
  229.5 8.1 convolution_convert_fusion
  237.6 7.4 gather_fusion.1
  245.1 7.4 gather_fusion
  252.9 24.1 %all-reduce.16.cloned.1.call-done = (bf16[1024,768]{1,0:T(8,128)(2,1)}, bf16[1024,768]{1,0:T(8,128)(2,1)}) async-done(((bf16[1024,768]{1,0:T(8,128)(2,1)}, bf16[1024,768]{1,0:T(8,128)(2,1)}), (bf16[1024,768]{1,0:T(8,128)(2,1)}, bf16[1024,768]{1,0:T(8,128)(2,1)})) %all-reduce.16.cloned.1.call-update) | async-done | bytes 3145744 | tf_op jit(solution)/shard_map/psum | solution.py:169
  277.0 2.5 fusion.63
  279.9 4.1 multiply_reduce_fusion.1
  284.0 2.5 convert_add_fusion
  289.8 15.9 %multiply_reduce_fusion = (f32[6,1024]{1,0:T(8,128)S(1)}, f32[6,1024,1024]{2,1,0:T(8,128)}) fusion(f32[6,1024,1024]{2,1,0:T(8,128)} %get-tuple-element.177, f32[6,1024]{1,0:T(8,128)S(1)} %log_add_fusion, bf16[1024,6,64]{0,2,1:T(8,128)(2,1)} %bitcast.187, bf16[1024,6,64]{0,2,1:T(8,128)(2,1)} %bitcast.198), kind=kOutput, calls=%fused_computation.23 | convolution fusion | flops 824174592 | bytes 51953664 | tf_op jit(solution)/shard_map/while/body/eval_jaxpr/ihd,jhd->hij/dot_general | solution.py:217
  305.8 25.6 %subtract_multiply_fusion = f32[6,1024,1024]{2,1,0:T(8,128)} fusion(f32[6,1024,1024]{2,1,0:T(8,128)} %get-tuple-element.184, f32[6,1024,1024]{2,1,0:T(8,128)} %get-tuple-element.177, f32[6,1024]{1,0:T(8,128)S(1)} %get-tuple-element.183, f32[6,1024]{1,0:T(8,128)S(1)} %log_add_fusion), kind=kLoop, calls=%fused_computation.22 | loop fusion | flops 18874368 | bytes 75546624 | tf_op jit(solution)/shard_map/while/body/eval_jaxpr/mul | solution.py:224
  331.4 13.2 multiply_convert_fusion.2
  344.6 11.7 multiply_convert_fusion.1
  356.2 11.5 fusion.94
  367.8 6.1 fusion.64
  373.9 2.3 copy.41
  376.2 2.3 copy.42
  378.5 2.3 copy.43
  380.8 5.0 bitcast_convert_fusion
  385.9 5.6 convolution_bitcast_fusion
  391.5 6.3 copy.45
  397.9 4.2 fusion.100
  402.3 12.2 fusion.111
  414.5 11.8 fusion.118
  428.2 28.0 %copy.53 = f32[6,8,128,1024]{3,0,2,1:T(8,128)} copy(f32[6,8,128,1024]{3,2,1,0:T(8,128)} %bitcast.178) | data formatting | bytes 50331648 | tf_op jit(solution)/shard_map/reshape | solution.py:59
  456.2 86.5 %while.5 = (s32[]{:T(128)}, f32[8,32,6]{1,2,0:T(8,128)S(1)}, s32[8,128,1024]{2,1,0:T(8,128)}, f32[8,6,128,1024]{3,1,2,0:T(8,128)}, s32[]{:T(128)}) while((s32[]{:T(128)}, f32[8,32,6]{1,2,0:T(8,128)S(1)}, s32[8,128,1024]{2,1,0:T(8,128)}, f32[8,6,128,1024]{3,1,2,0:T(8,128)}, s32[]{:T(128)}) %tuple.79), condition=%wide.region_24.25_spmd, body=%wide.region_23.24_spmd.sunk | while | flops 306184192 | bytes 5772353 | solution.py:72
  457.3 9.7 fusion.150
  468.1 9.7 fusion.150
  478.9 9.7 fusion.150
  489.8 9.7 fusion.150
  500.6 9.7 fusion.150
  511.4 9.7 fusion.150
  522.2 9.7 fusion.150
  533.0 9.7 fusion.150
  544.2 2.8 fusion.61
  547.0 78.9 %all-reduce.3 = (f32[768]{0:T(1024)S(1)}, f32[32,6]{0,1:T(8,128)}, f32[768]{0:T(1024)S(1)}) all-reduce(f32[768]{0:T(1024)S(1)} %get-tuple-element.142, f32[32,6]{0,1:T(8,128)S(1)} %reduce_sum.120, f32[768]{0:T(1024)S(1)} %get-tuple-element.140), channel_id=2, replica_groups=mesh['dp'=16,'tensor'=2] {'dp'}, use_global_device_ids=true, to_apply=%region_20.21.clone | all-reduce | flops 1728 | bytes 13824
  627.1 4.0 fusion.50
  631.0 74.7 %all-reduce.14.cloned.1.call-done = f32[3,768,384]{2,0,1:T(4,128)} async-done(((f32[3,768,384]{2,0,1:T(4,128)}), f32[3,768,384]{2,0,1:T(4,128)}) %all-reduce.14.cloned.1.call-update) | async-done | bytes 3538960
  707.5 126.8 %reduce-scatter.7.cloned.1.call-done = f32[384,48]{0,1:T(8,128)} async-done(((f32[384,768]{0,1:T(8,128)}), f32[384,48]{0,1:T(8,128)}) %reduce-scatter.7.cloned.1.call-update) | async-done | bytes 73744 | tf_op jit(solution)/shard_map/reduce_scatter | solution.py:269
  834.3 291.1 %reduce-scatter.11.cloned.1.call-done = f32[4,1536,48]{1,2,0:T(8,128)} async-done(((f32[4,1536,768]{1,2,0:T(8,128)}), f32[4,1536,48]{1,2,0:T(8,128)}) %reduce-scatter.11.cloned.1.call-update) | async-done | bytes 1179664 | tf_op jit(solution)/shard_map/reduce_scatter | solution.py:271
  1125.4 291.0 %reduce-scatter.9.cloned.1.call-done = f32[4,48,1536]{2,1,0:T(8,128)} async-done(((f32[4,768,1536]{2,1,0:T(8,128)}), f32[4,48,1536]{2,1,0:T(8,128)}) %reduce-scatter.9.cloned.1.call-update) | async-done | bytes 1179664 | tf_op jit(solution)/shard_map/reduce_scatter | solution.py:270
  (118 shorter events, 31.9 us)
Async XLA Ops:
  7.2 2.6 copy-start
  7.2 167.1 %all-reduce.10.cloned.1.call-start = ((), (), s32[]{:S(2)}) async-start(), calls=%async_computation.4 | async-start | bytes 3145728 | tf_op jit(solution)/shard_map/psum | solution.py:145
  9.8 3.6 copy-start.15
  14.5 95.6 %copy-start.8 = (bf16[1,1024,384]{1,2,0:T(8,128)(2,1)}, bf16[1,1024,384]{1,2,0:T(8,128)(2,1)S(1)}, u32[]{:S(2)}) copy-start(bf16[1,1024,384]{1,2,0:T(8,128)(2,1)S(1)} %get-tuple-element.170) | copy-start | bytes 2359300
  14.5 95.6 %copy-start.9 = (bf16[1,1024,384]{1,2,0:T(8,128)(2,1)}, bf16[1,1024,384]{1,2,0:T(8,128)(2,1)S(1)}, u32[]{:S(2)}) copy-start(bf16[1,1024,384]{1,2,0:T(8,128)(2,1)S(1)} %get-tuple-element.169) | copy-start | bytes 2359300
  14.5 5.8 copy-start.25
  82.0 26.5 %copy-start.17 = (s32[1,1024]{1,0:T(1,128)S(1)}, s32[1,1024]{1,0:T(1,128)}, u32[]{:S(2)}) copy-start(s32[1,1024]{1,0:T(1,128)} %param.26) | copy-start | bytes 12292
  126.0 11.4 copy-start.11
  137.5 11.4 copy-start.13
  147.9 1.0 copy-start.12
  147.9 3.2 copy-start.20
  147.9 3.2 copy-start.22
  147.9 26.4 %copy-start.1 = (bf16[1,1024,768]{2,1,0:T(8,128)(2,1)S(1)}, bf16[1,1024,768]{2,1,0:T(8,128)(2,1)}, u32[]{:S(2)}) copy-start(bf16[1,1024,768]{2,1,0:T(8,128)(2,1)} %param.17) | copy-start | bytes 4718596
  151.0 25.4 %copy-start.21 = (f32[768]{0:T(1024)S(1)}, f32[768]{0:T(1024)}, u32[]{:S(2)}) copy-start(f32[768]{0:T(1024)} %param.22) | copy-start | bytes 9220
  151.0 25.4 %copy-start.24 = (f32[768,4]{0,1:T(4,128)S(1)}, f32[768,4]{0,1:T(4,128)}, u32[]{:S(2)}) copy-start(f32[768,4]{0,1:T(4,128)} %param.23) | copy-start | bytes 36868
  151.0 126.0 %all-reduce.16.cloned.1.call-start = ((), (), s32[]{:S(2)}) async-start(), calls=%async_computation.11 | async-start | bytes 6291456 | tf_op jit(solution)/shard_map/psum | solution.py:169
  174.3 2.1 copy-start.4
  206.2 23.3 %slice-start = ((s8[9437184]{0:T(1024)(128)(4,1)}), s8[4194304]{0:T(1024)(128)(4,1)S(1)}, s32[]{:S(2)}) async-start(s8[9437184]{0:T(1024)(128)(4,1)} %bitcast.185), calls=%async_computation.12 | async-start | bytes 8388608
  206.2 23.3 %slice-start.1 = ((s8[9437184]{0:T(1024)(128)(4,1)}), s8[4194304]{0:T(1024)(128)(4,1)S(1)}, s32[]{:S(2)}) async-start(s8[9437184]{0:T(1024)(128)(4,1)} %bitcast.185), calls=%async_computation.13 | async-start | bytes 8388608
  220.0 9.5 slice-start.2
  252.4 290.3 %reduce-scatter.13.cloned.1.call-start = ((), (), s32[]{:S(2)}) async-start(), calls=%async_computation.9 | async-start | bytes 417792
  277.0 2.5 copy-start.5
  277.0 2.8 copy-start.23
  279.8 4.1 copy-start.3
  279.9 4.1 copy-start.10
  284.0 4.2 copy-start.14
  286.5 1.7 copy-start.2
  344.6 11.7 copy-start.7
  356.2 11.5 copy-start.6
  373.9 170.3 %all-reduce.12.cloned.1.call-start = ((), (), s32[]{:S(2)}) async-start(), calls=%async_computation.5 | async-start | bytes 3145728 | tf_op jit(solution)/shard_map/psum | solution.py:253
  380.8 5.1 copy-start.16
  380.8 5.1 copy-start.18
  385.9 319.9 %all-reduce.14.cloned.1.call-start = ((), (), s32[]{:S(2)}) async-start(), calls=%async_computation.10 | async-start | bytes 9437184
  397.9 436.4 %reduce-scatter.7.cloned.1.call-start = ((), (), s32[]{:S(2)}) async-start(), calls=%async_computation.6 | async-start | bytes 1253376 | tf_op jit(solution)/shard_map/reduce_scatter | solution.py:269
  402.2 723.2 %reduce-scatter.11.cloned.1.call-start = ((), (), s32[]{:S(2)}) async-start(), calls=%async_computation.8 | async-start | bytes 20054016 | tf_op jit(solution)/shard_map/reduce_scatter | solution.py:271
  414.5 1001.9 %reduce-scatter.9.cloned.1.call-start = ((), (), s32[]{:S(2)}) async-start(), calls=%async_computation.7 | async-start | bytes 20054016 | tf_op jit(solution)/shard_map/reduce_scatter | solution.py:270
  426.3 0.7 copy-start.26
  542.7 84.4 %copy-start.19 = (f32[1024]{0:T(1024)S(1)}, f32[1024]{0:T(1024)}, u32[]{:S(2)}) copy-start(f32[1024]{0:T(1024)} %get-tuple-element.172) | copy-start | bytes 12292
Sparse Core Ops, SparseCore 0:
  151.2 23.0 all-reduce.9
  252.6 24.4 all-reduce.15
  374.0 122.8 reduce-scatter.12
  499.2 19.4 all-reduce.11
  524.3 181.4 all-reduce.13
  711.6 122.5 reduce-scatter.6
  841.6 283.7 reduce-scatter.10
  1132.7 283.6 reduce-scatter.8
where the time goes:
time: 1430 us; the launch traced here: 1420 us
  waiting for transfers between devices  831 us (58%)
  matrix products  311 us (22%)
  local copies, waits for them, and re-layouts  110 us (8%)
  blocking collectives  78.9 us (6%)
  other arithmetic  76.8 us (5%)
  between operations  15.4 us (1%)
    reduce_scatter x1, waiting for transfers between devices, body(): lax.psum_scatter(grad_expert_out, 'dp', scatter_dimension=2, tiled=True)  291 us
    reduce_scatter x1, waiting for transfers between devices, body(): lax.psum_scatter(grad_expert_in, 'dp', scatter_dimension=1, tiled=True)  291 us
    reduce_scatter x1, waiting for transfers between devices, body(): lax.psum_scatter(grad_attn_out, 'dp', scatter_dimension=1, tiled=True)  127 us
    unnamed x1, blocking collectives  78.9 us
    dot_general x8, matrix products, table_one_rows(): jnp.einsum('hij,ijb->bh', score_piece, bucket_onehot(bucket_rows, count),...  77.7 us
    unnamed x10, waiting for transfers between devices  74.9 us
    dot_general x8, matrix products, expand_one_rows(): jnp.einsum('ijb,bh->hij', bucket_onehot(bucket_rows, count), table, preci...  52.9 us
  transfers between devices with their start and end apart: 8, of which 6 were waited for; matrix products, arithmetic and copies ran while one was open for 13% of the time, Pallas kernels for 0%

commit v1 on v0

v1 whole, which is shorter than its diff:
```python
import functools

import jax
import jax.numpy as jnp
from jax import lax
from jax.experimental import pallas as pl
from jax.experimental.pallas import tpu as pltpu
from jax.sharding import PartitionSpec as P

HEAD_DIM = 64
CAP = 320
EPS = 1e-06
NEG = -1e30
HIGH = lax.Precision.HIGHEST
BLOCK = 128
LIMIT = 48 * 1024 * 1024
F32 = jnp.float32
BF16 = jnp.bfloat16


def band_bucket():
    row = lax.broadcasted_iota(jnp.int32, (BLOCK, 5 * BLOCK), 0)
    column = lax.broadcasted_iota(jnp.int32, (BLOCK, 5 * BLOCK), 1)
    offset = column - 2 * BLOCK - row
    distance = jnp.abs(offset)
    coarse = jnp.full_like(distance, 8)
    for limit in (12, 16, 23, 32, 46, 64, 91):
        coarse = coarse + (distance >= limit).astype(jnp.int32)
    bucket = jnp.where(distance < 8, distance, coarse)
    return bucket + 16 * (offset > 0).astype(jnp.int32)


def band_bias(table, bucket):
    result = jnp.zeros((table.shape[1],) + bucket.shape, F32)
    for index in range(table.shape[0]):
        result = jnp.where(bucket[None] == index, table[index][:, None, None], result)
    return result


def band_table_grad(band, bucket, count):
    rows = [
        jnp.sum(jnp.where(bucket[None] == index, band, 0.0), axis=(1, 2)) for index in range(count)
    ]
    return jnp.stack(rows)


def row_norm(values, gain):
    inverse = lax.rsqrt(jnp.mean(values * values, axis=-1, keepdims=True) + EPS)
    return (values * inverse * gain, inverse)


def norm_back(grad_out, values, inverse, gain):
    scaled = grad_out * gain
    grad_gain = jnp.sum(grad_out * values * inverse, axis=0)
    grad_in = inverse * scaled - values * inverse**3 * jnp.mean(
        scaled * values, axis=-1, keepdims=True
    )
    return (grad_in, grad_gain)


def dot_t(left, right):
    return lax.dot_general(left, right, (((1,), (1,)), ((), ())), preferred_element_type=F32)


def dot_n(left, right):
    return lax.dot_general(left, right, (((1,), (0,)), ((), ())), preferred_element_type=F32)


def t_dot(left, right):
    return lax.dot_general(left, right, (((0,), (0,)), ((), ())), preferred_element_type=F32)


def bias_row(bias_ref, head, place, tiles):
    parts = []
    for tile in range(tiles):
        start = (jnp.clip(tile - place, -2, 2) + 2) * BLOCK
        parts.append(bias_ref[head, :, pl.ds(pl.multiple_of(start, BLOCK), BLOCK)])
    return jnp.concatenate(parts, axis=1)


def lane_half(array, head):
    lane = lax.broadcasted_iota(jnp.int32, array.shape, 1)
    return jnp.where((lane >= HEAD_DIM) == (head == 1), array, jnp.zeros_like(array))


def attend_kernel(q_ref, k_ref, v_ref, bias_ref, seg_col_ref, seg_row_ref, out_ref):
    place = pl.program_id(1)
    tiles = k_ref.shape[1] // BLOCK
    query, keys, values = q_ref[0], k_ref[0], v_ref[0]
    same = seg_col_ref[...] == seg_row_ref[...]
    total = None
    for head in range(2):
        raw = dot_t(lane_half(query, head), keys) * (HEAD_DIM**-0.5)
        scores = jnp.where(same, raw + bias_row(bias_ref, head, place, tiles), NEG)
        expo = jnp.exp(scores - jnp.max(scores, axis=-1, keepdims=True))
        probs = expo * (1.0 / jnp.sum(expo, axis=-1, keepdims=True))
        mixed = lane_half(dot_n(probs.astype(BF16), values), head)
        total = mixed if total is None else total + mixed
    out_ref[...] = total.astype(BF16)


def attend_back_kernel(
    q_ref, k_ref, v_ref, bias_ref, seg_col_ref, seg_row_ref, grad_ref, out_ref, band_ref, dk_ref, dv_ref
):
    place = pl.program_id(1)
    tiles = k_ref.shape[1] // BLOCK
    scale = HEAD_DIM**-0.5

    @pl.when(place == 0)
    def _():
        dk_ref[...] = jnp.zeros_like(dk_ref)
        dv_ref[...] = jnp.zeros_like(dv_ref)
        band_ref[...] = jnp.zeros_like(band_ref)

    query, keys, values, grad = q_ref[0], k_ref[0], v_ref[0], grad_ref[...]
    same = seg_col_ref[...] == seg_row_ref[...]
    dq = None
    for head in range(2):
        query_h, grad_h = lane_half(query, head), lane_half(grad, head)
        raw = dot_t(query_h, keys) * scale
        scores = jnp.where(same, raw + bias_row(bias_ref, head, place, tiles), NEG)
        expo = jnp.exp(scores - jnp.max(scores, axis=-1, keepdims=True))
        probs = expo * (1.0 / jnp.sum(expo, axis=-1, keepdims=True))
        grad_probs = dot_t(grad_h, values)
        inner = jnp.sum(grad_probs * probs, axis=-1, keepdims=True)
        grad_scores = probs * (grad_probs - inner)
        for tile in range(tiles):
            start = (jnp.clip(tile - place, -2, 2) + 2) * BLOCK
            band_ref[head, :, pl.ds(pl.multiple_of(start, BLOCK), BLOCK)] += grad_scores[
                :, tile * BLOCK : (tile + 1) * BLOCK
            ]
        low = grad_scores.astype(BF16)
        dv_ref[...] += t_dot(probs.astype(BF16), grad_h)
        dk_ref[...] += t_dot(low, query_h)
        part = lane_half(dot_n(low, keys), head)
        dq = part if dq is None else dq + part
    rows = pl.ds(pl.multiple_of(place * BLOCK, BLOCK), BLOCK)
    out_ref[0, rows, :] = (dq * scale).astype(BF16)

    @pl.when(place == tiles - 1)
    def _():
        out_ref[1] = (dk_ref[...] * scale).astype(BF16)
        out_ref[2] = dv_ref[...].astype(BF16)


def attention_specs(length):
    return [
        pl.BlockSpec((1, BLOCK, BLOCK), lambda p, i: (0, i, p)),
        pl.BlockSpec((1, length, BLOCK), lambda p, i: (1, 0, p)),
        pl.BlockSpec((1, length, BLOCK), lambda p, i: (2, 0, p)),
        pl.BlockSpec((2, BLOCK, 5 * BLOCK), lambda p, i: (p, 0, 0)),
        pl.BlockSpec((BLOCK, 1), lambda p, i: (i, 0)),
        pl.BlockSpec((1, length), lambda p, i: (0, 0)),
    ]


def attend(projected, bias, segment):
    _, length, width = projected.shape
    pairs = width // BLOCK
    return pl.pallas_call(
        attend_kernel,
        grid=(pairs, length // BLOCK),
        in_specs=attention_specs(length),
        out_specs=pl.BlockSpec((BLOCK, BLOCK), lambda p, i: (i, p)),
        out_shape=jax.ShapeDtypeStruct((length, width), BF16),
        compiler_params=pltpu.CompilerParams(vmem_limit_bytes=LIMIT),
        cost_estimate=pl.CostEstimate(
            flops=16 * length * length * width, bytes_accessed=8 * length * width, transcendentals=6 * length * length
        ),
    )(projected, projected, projected, bias, segment[:, None], segment[None, :])


def attend_back(projected, bias, segment, grad):
    _, length, width = projected.shape
    pairs = width // BLOCK
    return pl.pallas_call(
        attend_back_kernel,
        grid=(pairs, length // BLOCK),
        in_specs=attention_specs(length) + [pl.BlockSpec((BLOCK, BLOCK), lambda p, i: (i, p))],
        out_specs=[
            pl.BlockSpec((3, length, BLOCK), lambda p, i: (0, 0, p)),
            pl.BlockSpec((2, BLOCK, 5 * BLOCK), lambda p, i: (p, 0, 0)),
        ],
        out_shape=[
            jax.ShapeDtypeStruct((3, length, width), BF16),
            jax.ShapeDtypeStruct((2 * pairs, BLOCK, 5 * BLOCK), F32),
        ],
        scratch_shapes=[pltpu.VMEM((length, BLOCK), F32), pltpu.VMEM((length, BLOCK), F32)],
        compiler_params=pltpu.CompilerParams(vmem_limit_bytes=LIMIT),
        cost_estimate=pl.CostEstimate(
            flops=48 * length * length * width, bytes_accessed=16 * length * width, transcendentals=6 * length * length
        ),
    )(projected, projected, projected, bias, segment[:, None], segment[None, :], grad)


def pair_sum(part, size):
    if size != 2:
        return lax.psum(part.astype(F32), "tensor")
    other = lax.ppermute(part, "tensor", [(0, 1), (1, 0)])
    return part.astype(F32) + other.astype(F32)


def bits_of(size):
    bits = size.bit_length() - 1
    assert 1 << bits == size
    return bits


def swap(array, size, bit):
    return lax.ppermute(array, "dp", [(i, i ^ (1 << bit)) for i in range(size)])


def scatter_sum(unit, size, order):
    bits = bits_of(size)
    rows, columns = unit.shape
    me = lax.axis_index("dp")
    held = unit.reshape((2,) * bits + (rows // size, columns))
    left = list(range(bits - 1, -1, -1))
    for step, bit in enumerate(order):
        axis = left.index(bit)
        mine = (me >> bit) & 1
        sent = lax.dynamic_index_in_dim(held, 1 - mine, axis, keepdims=False)
        kept = lax.dynamic_index_in_dim(held, mine, axis, keepdims=False)
        got = swap(sent, size, bit)
        held = kept.astype(F32) + got.astype(F32)
        if step < bits - 1:
            held = held.astype(BF16)
        left.remove(bit)
    return held


def small_sum(array, size):
    for bit in range(bits_of(size)):
        array = array + swap(array, size, bit)
    return array


def orders_of(size):
    bits = bits_of(size)
    if bits == 4:
        return [(0, 1, 2, 3), (1, 0, 2, 3), (2, 0, 1, 3)]
    return [tuple(range(bits)), tuple(range(bits - 1, -1, -1)), tuple(range(bits))]


def body(
    dp,
    tp,
    tokens,
    gain_attn,
    query_key_value_weight,
    attn_out_weight,
    position_bias_matrix,
    gain_expert,
    router,
    expert_in,
    expert_out,
    segments,
    routes,
    slots,
    cotangent,
):
    seqs, length, width = tokens.shape
    count = seqs * length
    experts = expert_in.shape[0]
    places = experts * CAP
    local = attn_out_weight.shape[0]
    orders = orders_of(dp)
    inputs = tokens.astype(F32).reshape(count, width)
    normed_a, inverse_a = row_norm(inputs, gain_attn)
    act_a = normed_a.astype(BF16)
    projected = jnp.einsum(
        "td,cde->cte", act_a, query_key_value_weight, preferred_element_type=F32
    ).astype(BF16)
    bucket = band_bucket()
    bias = band_bias(position_bias_matrix, bucket)
    per_seq = projected.reshape(3, seqs, length, local)
    flat_att = jnp.concatenate([attend(per_seq[:, s], bias, segments[s]) for s in range(seqs)], axis=0)
    attn_part = jnp.dot(flat_att, attn_out_weight, preferred_element_type=F32).astype(BF16)
    hidden_res = inputs + pair_sum(attn_part, tp)
    normed_e, inverse_e = row_norm(hidden_res, gain_expert)
    logits = jnp.dot(normed_e, router, precision=HIGH, preferred_element_type=F32)
    chance = jax.nn.softmax(logits, axis=-1)
    route_flat = routes.reshape(count)
    onehot = (route_flat[:, None] == jnp.arange(experts, dtype=jnp.int32)[None, :]).astype(F32)
    gate = jnp.sum(chance * onehot, axis=-1)
    block = jnp.arange(count, dtype=jnp.int32) // length
    place = (block * places) + route_flat * CAP + slots.reshape(count)
    spot = jnp.arange(seqs * places, dtype=jnp.int32)
    to_slot = (spot[:, None] == place[None, :]).astype(BF16)
    to_token = (place[:, None] == spot[None, :]).astype(BF16)
    act_e = normed_e.astype(BF16)
    upstream = cotangent.astype(F32).reshape(count, width)
    scaled_up = (upstream * gate[:, None]).astype(BF16)

    def dispatch(array):
        made = jnp.dot(to_slot, array, preferred_element_type=F32).astype(BF16)
        made = made.reshape(seqs, experts, CAP, width)
        return jnp.transpose(made, (1, 0, 2, 3)).reshape(experts, seqs * CAP, width)

    def collect(array):
        array = jnp.transpose(array.reshape(experts, seqs, CAP, width), (1, 0, 2, 3))
        array = array.reshape(seqs * places, width)
        return jnp.dot(to_token, array, preferred_element_type=F32).astype(BF16)

    dispatched = dispatch(act_e)
    slot_grad = dispatch(scaled_up)
    inner = jnp.einsum("ecd,edf->ecf", dispatched, expert_in, preferred_element_type=F32)
    activated = jax.nn.gelu(inner).astype(BF16)
    grad_out_t = [
        jnp.einsum("cd,cf->df", slot_grad[e], activated[e], preferred_element_type=F32).astype(BF16)
        for e in range(experts)
    ]
    summed_out = [scatter_sum(g, dp, orders[e % 2]) for e, g in enumerate(grad_out_t)]
    grad_act = jnp.einsum("ecd,efd->ecf", slot_grad, expert_out, preferred_element_type=F32)
    unused, gelu_pull = jax.vjp(jax.nn.gelu, inner)
    grad_inner = gelu_pull(grad_act)[0].astype(BF16)
    grad_in = [
        jnp.einsum("cd,cf->df", dispatched[e], grad_inner[e], preferred_element_type=F32).astype(BF16)
        for e in range(experts)
    ]
    summed_in = [scatter_sum(g, dp, orders[(2, 0, 1, 2)[e % 4]]) for e, g in enumerate(grad_in)]
    returned = jnp.einsum("ecf,efd->ecd", activated, expert_out, preferred_element_type=F32).astype(BF16)
    expert_total = pair_sum(collect(returned), tp)
    grad_disp = jnp.einsum("ecf,edf->ecd", grad_inner, expert_in, preferred_element_type=F32).astype(BF16)
    back_expert = pair_sum(collect(grad_disp), tp)
    output = (hidden_res + expert_total * gate[:, None]).astype(BF16).reshape(seqs, length, width)
    grad_gate = jnp.sum(upstream * expert_total, axis=-1)
    grad_logits = (grad_gate * gate)[:, None] * (onehot - chance)
    grad_router = jnp.dot(normed_e.T, grad_logits, precision=HIGH, preferred_element_type=F32)
    grad_normed_e = back_expert + jnp.dot(
        grad_logits, router.T, precision=HIGH, preferred_element_type=F32
    )
    grad_hidden_part, grad_gain_expert = norm_back(grad_normed_e, hidden_res, inverse_e, gain_expert)
    grad_hidden = upstream + grad_hidden_part
    grad_hidden_low = grad_hidden.astype(BF16)
    grad_attn_out_t = jnp.dot(grad_hidden_low.T, flat_att, preferred_element_type=F32).astype(BF16)
    grad_attended = jnp.dot(
        grad_hidden_low, attn_out_weight.T, preferred_element_type=F32
    ).astype(BF16)
    parts, bands = [], None
    for s in range(seqs):
        part, band = attend_back(
            per_seq[:, s], bias, segments[s], grad_attended.reshape(seqs, length, local)[s]
        )
        parts.append(part)
        bands = band if bands is None else bands + band
    grads = jnp.concatenate(parts, axis=1)
    weight_grads = [
        jnp.dot(act_a.T, grads[k], preferred_element_type=F32).astype(BF16) for k in range(3)
    ]
    last = scatter_sum(jnp.concatenate(weight_grads + [grad_attn_out_t], axis=1), dp, orders[0])
    grad_act_a = jnp.einsum("cte,cde->td", grads, query_key_value_weight, preferred_element_type=F32)
    grad_table = band_table_grad(bands, bucket, position_bias_matrix.shape[0])
    back_attn = pair_sum(grad_act_a.astype(BF16), tp)
    grad_in_part, grad_gain_attn = norm_back(back_attn, inputs, inverse_a, gain_attn)
    grad_tokens = (grad_hidden + grad_in_part).reshape(seqs, length, width)
    small = jnp.concatenate(
        [grad_gain_attn, grad_gain_expert, grad_router.T.reshape(-1), grad_table.reshape(-1)]
    )
    small = small_sum(small, dp)
    me = lax.axis_index("dp")
    share = width // dp
    wide = lax.dynamic_slice_in_dim(small[: 6 * width].reshape(6, width), me * share, share, axis=1)
    return (
        output,
        grad_tokens,
        wide[0],
        jnp.transpose(last[:, : 3 * local].reshape(share, 3, local), (1, 0, 2)),
        last[:, 3 * local :].T,
        small[6 * width :].reshape(position_bias_matrix.shape),
        wide[1],
        wide[2:].T,
        jnp.stack(summed_in),
        jnp.transpose(jnp.stack(summed_out), (0, 2, 1)),
    )


def solution(mesh):
    in_specs = (
        P("dp", None, None),
        P(),
        P(None, None, "tensor"),
        P("tensor", None),
        P(None, "tensor"),
        P(),
        P(),
        P(None, None, "tensor"),
        P(None, "tensor", None),
        P("dp", None),
        P("dp", None),
        P("dp", None),
        P("dp", None, None),
    )
    out_specs = (
        P("dp", None, None),
        P("dp", None, None),
        P("dp"),
        P(None, "dp", "tensor"),
        P("tensor", "dp"),
        P(None, "tensor"),
        P("dp"),
        P("dp", None),
        P(None, "dp", "tensor"),
        P(None, "tensor", "dp"),
    )
    run = functools.partial(body, mesh.shape["dp"], mesh.shape["tensor"])
    return jax.shard_map(run, mesh=mesh, in_specs=in_specs, out_specs=out_specs, check_vma=False)
```

time: 1430 us -> 490 us (0.34)
  waiting for transfers between devices: 831 us -> 150 us
  matrix products: 311 us -> 99.9 us
  blocking collectives: 78.9 us -> 0 us
  Pallas kernels: 0 us -> 74.1 us
  local copies, waits for them, and re-layouts: 110 us -> 41.5 us
  starting transfers between devices: 0.73 us -> 51 us
    reduce_scatter x3 -> x0, waiting for transfers between devices: 709 us -> none  [the longest x1 291 us: body(): lax.psum_scatter(grad_expert_out, 'dp', scatter_dimension=2, tiled=True)]
    dot_general x31 -> x22, matrix products: 259 us -> 52.7 us  [the longest x4 11.3 us: body(): jnp.einsum('cd,cf->df', dispatched[e], grad_inner[e], preferred_element_t...]
    ppermute x0 -> x44, waiting for transfers between devices: none -> 150 us  [the longest x40 149 us: swap(): return lax.ppermute(array, 'dp', [(i, i ^ 1 << bit) for i in range(size)])]
    unnamed x1 -> x0, blocking collectives: 78.9 us -> none
    unnamed x10 -> x0, waiting for transfers between devices: 74.9 us -> none
    pallas_call x0 -> x2, Pallas kernels: none -> 74.1 us  [the longest x1 46.9 us: attend_back(): pl.pallas_call(attend_back_kernel, grid=(pairs, length // BLOCK), in_spec...]
    ppermute x0 -> x44, starting transfers between devices: none -> 51 us  [the longest x40 49.9 us: swap(): return lax.ppermute(array, 'dp', [(i, i ^ 1 << bit) for i in range(size)])]
    psum x3 -> x0, waiting for transfers between devices: 47.3 us -> none  [the longest x1 24.1 us: body(): expert_total = lax.psum(returned[place], 'tensor').astype(jnp.float32)]
  transfers between devices with their start and end apart: 8 -> 44, of which waited for: 6 -> 26; matrix products, arithmetic and copies ran while one was open for 13% -> 19% of each run, Pallas kernels for 0% -> 10%
where the time goes in v1:
time: 490 us; the launch traced here: 485 us
  waiting for transfers between devices  150 us (31%)
  matrix products  99.9 us (20%)
  Pallas kernels  74.1 us (15%)
  other arithmetic  66.1 us (13%)
  starting transfers between devices  51 us (10%)
  local copies, waits for them, and re-layouts  41.5 us (8%)
    ppermute x40, waiting for transfers between devices, swap(): return lax.ppermute(array, 'dp', [(i, i ^ 1 << bit) for i in range(size)])  149 us
    ppermute x40, starting transfers between devices, swap(): return lax.ppermute(array, 'dp', [(i, i ^ 1 << bit) for i in range(size)])  49.9 us
    pallas_call x1, Pallas kernels, attend_back(): pl.pallas_call(attend_back_kernel, grid=(pairs, length // BLOCK), in_spec...  46.9 us
    pallas_call x1, Pallas kernels, attend(): pl.pallas_call(attend_kernel, grid=(pairs, length // BLOCK), in_specs=att...  27.2 us
    select_n x1, other arithmetic, band_bias(): jnp.where(bucket[None] == index, table[index][:, None, None], result)  19.3 us
    unnamed x264, local copies, waits for them, and re-layouts  16 us
    convert_element_type x27, other arithmetic, scatter_sum(): held = held.astype(BF16)  15.5 us
    dot_general x1, matrix products, body(): jnp.einsum('ecd,edf->ecf', dispatched, expert_in, preferred_element_type=...  14.2 us
  transfers between devices with their start and end apart: 44, of which 26 were waited for; matrix products, arithmetic and copies ran while one was open for 19% of the time, Pallas kernels for 10%

profile of v1, /device:TPU:0, one launch (start us, length us, event | category | flops | bytes accessed | tf_op | source)
XLA Modules:
  0.0 485.4 jit_solution(15544038575804703918)
XLA Ops:
  2.2 2.5 slice_reduce_fusion.31
  4.7 2.6 copy.141
  7.4 1.8 fusion.19
  9.8 2.9 broadcast_compare_fusion.26
  13.3 4.0 convert_bitcast_fusion.1.q_ref.k_ref.v_ref
  17.7 19.3 %select_select_fusion.bias_ref = f32[6,128,640]{2,1,0:T(8,128)S(1)} fusion(f32[6]{0:T(128)S(1)} %get-tuple-element.120, f32[6]{0:T(128)S(1)} %get-tuple-element.121, f32[6]{0:T(128)S(1)} %get-tuple-element.91, f32[6]{0:T(128)S(1)} %get-tuple-element.92, f32[6]{0:T(128)S(1)} %get-tuple-element.93, f32[6]{0:T(128)S(1)} %get-tuple-element.94, ...), kind=kLoop, calls=%fused_computation.120 | loop fusion | flops 15728640 | bytes 4588288 | tf_op jit(solution)/shard_map/jit(_where)/select_n | solution.py:36
  37.0 27.2 %shard_map.204 = bf16[1024,384]{1,0:T(8,128)(2,1)S(1)} custom-call(bf16[3,1024,384]{2,1,0:T(8,128)(2,1)S(1)} %convert_bitcast_fusion.1.q_ref.k_ref.v_ref, bf16[3,1024,384]{2,1,0:T(8,128)(2,1)S(1)} %convert_bitcast_fusion.1.q_ref.k_ref.v_ref, bf16[3,1024,384]{2,1,0:T(8,128)(2,1)S(1)} %convert_bitcast_fusion.1.q_ref.k_ref.v_ref, ...), custom_call_target="tpu_custom_call" | custom-call | flops 6442450944 | bytes 3145728 | tf_op jit(solution)/shard_map/pallas_call | solution.py:160
  64.2 2.2 convolution_convert_fusion.10
  66.9 2.6 copy.144
  70.2 3.4 multiply_reduce_fusion.2
  73.7 2.0 fusion.141
  75.8 2.6 fusion.17
  78.4 2.5 fusion.18
  81.0 12.8 %fusion.142 = f32[4,320,1536]{2,1,0:T(8,128)} fusion(bf16[4,320,768]{2,1,0:T(8,128)(2,1)S(1)} %bitcast.398, bf16[4,1536,768]{2,1,0:T(8,128)(2,1)} %param.21), kind=kOutput, calls=%fused_computation.401 | convolution fusion | flops 3019898880 | bytes 19267584 | tf_op jit(solution)/shard_map/ecd,efd->ecf/dot_general | solution.py:314
  93.7 14.2 %fusion.6 = (bf16[4,320,1536]{2,1,0:T(8,128)(2,1)}, bf16[4,320,1536]{2,1,0:T(8,128)(2,1)}) fusion(f32[4,320,1536]{2,1,0:T(8,128)} %fusion.142, bf16[4,320,768]{2,1,0:T(8,128)(2,1)S(1)} %bitcast.454, bf16[4,768,1536]{2,1,0:T(8,128)(2,1)} %param.20), kind=kOutput, calls=%fused_computation.8 | convolution fusion | flops 3063152640 | bytes 27131904 | tf_op jit(solution)/shard_map/ecd,edf->ecf/dot_general | solution.py:307
  107.9 9.4 %convolution_convert_fusion.8 = bf16[4,320,768]{2,1,0:T(8,128)(2,1)} fusion(bf16[4,320,1536]{2,1,0:T(8,128)(2,1)} %get-tuple-element.126, bf16[4,768,1536]{2,1,0:T(8,128)(2,1)} %param.20), kind=kOutput, calls=%fused_computation.121 | convolution fusion | flops 3020881920 | bytes 15335424 | tf_op jit(solution)/shard_map/ecf,edf->ecd/dot_general | solution.py:324
  117.3 2.8 convolution_convert_fusion.4
  120.1 2.8 convolution_convert_fusion.7
  122.9 2.8 convolution_convert_fusion.5
  125.7 2.9 convolution_convert_fusion.6
  128.7 6.9 %convolution_convert_fusion.9 = bf16[4,320,768]{2,1,0:T(8,128)(2,1)S(1)} fusion(bf16[4,320,1536]{2,1,0:T(8,128)(2,1)S(1)} %copy-done.126, bf16[4,1536,768]{2,1,0:T(8,128)(2,1)} %param.21), kind=kOutput, calls=%fused_computation.122 | convolution fusion | flops 3020881920 | bytes 15335424 | tf_op jit(solution)/shard_map/ecf,efd->ecd/dot_general | solution.py:322
  140.0 2.5 fusion.50
  143.0 3.6 fusion.51
  148.2 2.9 collective-permute-start.24
  157.1 2.8 convolution_convert_fusion.3
  160.7 17.0 %collective-permute-done.24 = bf16[2,2,2,48,1536]{4,3,0,1,2:T(8,128)(2,1)} collective-permute-done((bf16[2,2,2,48,1536]{4,3,0,1,2:T(8,128)(2,1)}, bf16[2,2,2,48,1536]{4,3,0,1,2:T(8,128)(2,1)}, u32[]{:S(2)}, u32[]{:S(2)}) %collective-permute-start.24) | collective-permute-done | bytes 1179680 | tf_op jit(solution)/shard_map/ppermute | solution.py:210
  177.8 1.7 collective-permute-start.12
  187.3 17.9 %collective-permute-done.12 = bf16[2,2,2,48,1536]{4,3,0,1,2:T(8,128)(2,1)S(1)} collective-permute-done((bf16[2,2,2,48,1536]{4,3,0,1,2:T(8,128)(2,1)S(1)}, bf16[2,2,2,48,1536]{4,3,0,1,2:T(8,128)(2,1)S(1)}, u32[]{:S(2)}, u32[]{:S(2)}) %collective-permute-start.12) | collective-permute-done | bytes 1179680 | tf_op jit(solution)/shard_map/ppermute | solution.py:210
  209.4 2.0 collective-permute-start.28
  214.1 19.3 %collective-permute-done.32 = bf16[2,2,2,48,1536]{4,3,0,1,2:T(8,128)(2,1)S(1)} collective-permute-done((bf16[2,2,2,48,1536]{4,3,0,1,2:T(8,128)(2,1)S(1)}, bf16[2,2,2,48,1536]{4,3,0,1,2:T(8,128)(2,1)S(1)}, u32[]{:S(2)}, u32[]{:S(2)}) %collective-permute-start.32) | collective-permute-done | bytes 1179680 | tf_op jit(solution)/shard_map/ppermute | solution.py:210
  245.8 5.6 %multiply_reduce_fusion = (f32[768]{0:T(1024)S(1)}, f32[1024]{0:T(1024)S(1)}, f32[1024,768]{0,1:T(8,128)S(1)}) fusion(f32[1024,768]{0,1:T(8,128)S(1)} %get-tuple-element.125, f32[1024]{0:T(1024)S(1)} %get-tuple-element.151, f32[768]{0:T(1024)S(1)} %copy-done.92, f32[768,4]{0,1:T(4,128)S(1)} %copy-done.93, f32[1024,4]{0,1:T(4,128)S(1)} %get-tuple-element.123, ...), kind=kOutput, calls=%fused_computation.52 | convolution fusion | flops 45627648 | bytes 9488384 | tf_op jit(solution)/shard_map/dot_general | solution.py:330
  251.5 3.0 convert_add_fusion
  257.2 46.9 %shard_map.205 = (bf16[3,1024,384]{2,1,0:T(8,128)(2,1)}, f32[6,128,640]{2,1,0:T(8,128)S(1)}) custom-call(bf16[3,1024,384]{2,1,0:T(8,128)(2,1)} %copy-done.4, bf16[3,1024,384]{2,1,0:T(8,128)(2,1)} %copy-done.4, bf16[3,1024,384]{2,1,0:T(8,128)(2,1)} %copy-done.4, f32[6,128,640]{2,1,0:T(8,128)S(1)} %copy-done.2, s32[1024,1]{1,0:T(8,128)S(1)} %copy.143.seg_col_ref, ...), custom_call_target="tpu_custom_call" | custom-call | flops 19327352832 | bytes 6291456 | tf_op jit(solution)/shard_map/pallas_call | solution.py:176
  304.4 4.4 select_reduce_fusion.18
  308.9 5.8 %select_reduce_fusion = (f32[6]{0:T(128)}, f32[6]{0:T(128)}, f32[6]{0:T(128)}, f32[6]{0:T(128)}, f32[6]{0:T(128)}, /*index=5*/f32[6]{0:T(128)}, f32[6]{0:T(128)}...) fusion(f32[6,128,640]{2,1,0:T(8,128)S(1)} %get-tuple-element.13, ...), kind=kLoop, calls=%fused_computation.88 | loop fusion | flops 17694612 | bytes 3441072 | tf_op jit(solution)/shard_map/reduce_sum | solution.py:42
  316.3 3.4 bitcast_convert_fusion
  324.4 4.3 copy.149
  328.6 4.7 fusion.38
  334.6 2.8 copy.166
  348.9 5.5 %collective-permute-done.37 = bf16[2,2,48,1536]{3,2,0,1:T(8,128)(2,1)S(1)} collective-permute-done((bf16[2,2,48,1536]{3,2,0,1:T(8,128)(2,1)}, bf16[2,2,48,1536]{3,2,0,1:T(8,128)(2,1)S(1)}, u32[]{:S(2)}, u32[]{:S(2)}) %collective-permute-start.37) | collective-permute-done | bytes 589856 | tf_op jit(solution)/shard_map/ppermute | solution.py:210
  355.2 1.7 collective-permute-start.22
  357.1 9.2 %collective-permute-done.29 = bf16[2,2,48,1536]{3,2,0,1:T(8,128)(2,1)S(1)} collective-permute-done((bf16[2,2,48,1536]{3,2,0,1:T(8,128)(2,1)}, bf16[2,2,48,1536]{3,2,0,1:T(8,128)(2,1)S(1)}, u32[]{:S(2)}, u32[]{:S(2)}) %collective-permute-start.29) | collective-permute-done | bytes 589856 | tf_op jit(solution)/shard_map/ppermute | solution.py:210
  368.0 2.7 collective-permute-done.26
  372.3 3.9 collective-permute-done.18
  378.5 4.0 collective-permute-done.42
  384.0 6.4 %collective-permute-done.38 = bf16[2,48,1536]{2,1,0:T(8,128)(2,1)S(1)} collective-permute-done((bf16[2,48,1536]{2,1,0:T(8,128)(2,1)S(1)}, bf16[2,48,1536]{2,1,0:T(8,128)(2,1)S(1)}, u32[]{:S(2)}, u32[]{:S(2)}) %collective-permute-start.38) | collective-permute-done | bytes 294944 | tf_op jit(solution)/shard_map/ppermute | solution.py:210
  392.0 6.7 %collective-permute-done.34 = bf16[2,48,1536]{2,1,0:T(8,128)(2,1)S(1)} collective-permute-done((bf16[2,48,1536]{2,1,0:T(8,128)(2,1)S(1)}, bf16[2,48,1536]{2,1,0:T(8,128)(2,1)S(1)}, u32[]{:S(2)}, u32[]{:S(2)}) %collective-permute-start.34) | collective-permute-done | bytes 294944 | tf_op jit(solution)/shard_map/ppermute | solution.py:210
  398.8 1.9 collective-permute-start.23
  400.8 2.5 collective-permute-done.30
  404.0 2.5 collective-permute-start.15
  406.4 10.3 %collective-permute-done.23 = bf16[48,1536]{1,0:T(8,128)(2,1)S(1)} collective-permute-done((bf16[48,1536]{1,0:T(8,128)(2,1)S(1)}, bf16[48,1536]{1,0:T(8,128)(2,1)S(1)}, u32[]{:S(2)}, u32[]{:S(2)}) %collective-permute-start.23) | collective-permute-done | bytes 147488 | tf_op jit(solution)/shard_map/ppermute | solution.py:210
  416.8 6.3 %collective-permute-done.19 = bf16[48,1536]{1,0:T(8,128)(2,1)S(1)} collective-permute-done((bf16[48,1536]{1,0:T(8,128)(2,1)S(1)}, bf16[48,1536]{1,0:T(8,128)(2,1)S(1)}, u32[]{:S(2)}, u32[]{:S(2)}) %collective-permute-start.19) | collective-permute-done | bytes 147488 | tf_op jit(solution)/shard_map/ppermute | solution.py:210
  423.1 3.1 collective-permute-done.15
  426.3 6.3 %collective-permute-done.43 = bf16[48,1536]{1,0:T(8,128)(2,1)S(1)} collective-permute-done((bf16[48,1536]{1,0:T(8,128)(2,1)S(1)}, bf16[48,1536]{1,0:T(8,128)(2,1)S(1)}, u32[]{:S(2)}, u32[]{:S(2)}) %collective-permute-start.43) | collective-permute-done | bytes 147488 | tf_op jit(solution)/shard_map/ppermute | solution.py:210
  432.6 7.9 %collective-permute-done.39 = bf16[48,1536]{1,0:T(8,128)(2,1)S(1)} collective-permute-done((bf16[48,1536]{1,0:T(8,128)(2,1)S(1)}, bf16[48,1536]{1,0:T(8,128)(2,1)S(1)}, u32[]{:S(2)}, u32[]{:S(2)}) %collective-permute-start.39) | collective-permute-done | bytes 147488 | tf_op jit(solution)/shard_map/ppermute | solution.py:210
  446.4 1.9 collective-permute-start.4
  450.3 2.8 collective-permute-start.5
  455.1 3.8 collective-permute-done.6
  459.5 2.7 fusion.25
  462.3 3.5 copy.167
  467.9 2.1 collective-permute-start.10
  470.6 5.3 %collective-permute-done.10 = bf16[2,48,1536]{2,1,0:T(8,128)(2,1)S(1)} collective-permute-done((bf16[2,48,1536]{2,1,0:T(8,128)(2,1)S(1)}, bf16[2,48,1536]{2,1,0:T(8,128)(2,1)S(1)}, u32[]{:S(2)}, u32[]{:S(2)}) %collective-permute-start.10) | collective-permute-done | bytes 294944 | tf_op jit(solution)/shard_map/ppermute | solution.py:210
  476.1 2.6 collective-permute-start.11
  479.2 4.6 collective-permute-done.11
  (438 shorter events, 91.2 us)
Async XLA Ops:
  37.0 27.2 %copy-start.1 = (f32[6,128,640]{2,1,0:T(8,128)}, f32[6,128,640]{2,1,0:T(8,128)S(1)}, u32[]{:S(2)}) copy-start(f32[6,128,640]{2,1,0:T(8,128)S(1)} %select_select_fusion.bias_ref) | copy-start | bytes 5898244
  66.4 3.8 collective-permute-start
  73.7 177.8 %copy-start.5 = (f32[1024,768]{0,1:T(8,128)}, f32[1024,768]{0,1:T(8,128)S(1)}, u32[]{:S(2)}) copy-start(f32[1024,768]{0,1:T(8,128)S(1)} %get-tuple-element.125) | copy-start | bytes 9437188
  81.0 57.4 %copy-start.30 = (bf16[1280,768]{1,0:T(8,128)(2,1)}, bf16[1280,768]{1,0:T(8,128)(2,1)S(1)}, u32[]{:S(2)}) copy-start(bf16[1280,768]{1,0:T(8,128)(2,1)S(1)} %fusion.18) | copy-start | bytes 5898244
  142.5 100.1 %collective-permute-start.1 = (bf16[1024,768]{0,1:T(8,128)(2,1)S(1)}, bf16[1024,768]{0,1:T(8,128)(2,1)S(1)}, u32[]{:S(2)}, u32[]{:S(2)}) collective-permute-start(bf16[1024,768]{0,1:T(8,128)(2,1)S(1)} %fusion.50), channel_id=1, source_target_pairs={{0,1},{1,0},{2,3},{3,2},{4,5},{5,4},{6,7},{7,6},{8,9},{9,8},{10,11... | collective-permute-start | bytes 4718600 | tf_op jit(solution)/shard_map/ppermute | solution.py:199
  146.6 97.8 %collective-permute-start.2 = (bf16[1024,768]{0,1:T(8,128)(2,1)}, bf16[1024,768]{0,1:T(8,128)(2,1)}, u32[]{:S(2)}, u32[]{:S(2)}) collective-permute-start(bf16[1024,768]{0,1:T(8,128)(2,1)} %fusion.51), channel_id=1, source_target_pairs={{0,1},{1,0},{2,3},{3,2},{4,5},{5,4},{6,7},{7,6},{8,9},{9,8},{10,11... | collective-permute-start | bytes 4718600 | tf_op jit(solution)/shard_map/ppermute | solution.py:199
  148.2 29.5 %collective-permute-start.24 = (bf16[2,2,2,48,1536]{4,3,0,1,2:T(8,128)(2,1)}, bf16[2,2,2,48,1536]{4,3,0,1,2:T(8,128)(2,1)}, u32[]{:S(2)}, u32[]{:S(2)}) collective-permute-start(bf16[2,2,2,48,1536]{4,3,0,1,2:T(8,128)(2,1)} %bitcast.390), channel_id=1, source_target_pairs={{0,8},{2,10},{4,12},{6,14},{8,0},{10,2},{12,4},{14,6},{16,24},{18,... | collective-permute-start | bytes 3538952 | tf_op jit(solution)/shard_map/ppermute | solution.py:210
  152.4 28.6 %collective-permute-start.20 = (bf16[2,2,2,48,1536]{4,3,0,1,2:T(8,128)(2,1)}, bf16[2,2,2,48,1536]{4,3,0,1,2:T(8,128)(2,1)}, u32[]{:S(2)}, u32[]{:S(2)}) collective-permute-start(bf16[2,2,2,48,1536]{4,3,0,1,2:T(8,128)(2,1)} %bitcast.391), channel_id=1, source_target_pairs={{0,4},{2,6},{4,0},{6,2},{8,12},{10,14},{12,8},{14,10},{16,20},{18,... | collective-permute-start | bytes 3538952 | tf_op jit(solution)/shard_map/ppermute | solution.py:210
  155.3 29.0 %collective-permute-start.16 = (bf16[2,2,2,48,1536]{4,3,0,1,2:T(8,128)(2,1)}, bf16[2,2,2,48,1536]{4,3,0,1,2:T(8,128)(2,1)}, u32[]{:S(2)}, u32[]{:S(2)}) collective-permute-start(bf16[2,2,2,48,1536]{4,3,0,1,2:T(8,128)(2,1)} %bitcast.392), channel_id=1, source_target_pairs={{0,2},{2,0},{4,6},{6,4},{8,10},{10,8},{12,14},{14,12},{16,18},{18,... | collective-permute-start | bytes 3538952 | tf_op jit(solution)/shard_map/ppermute | solution.py:210
  177.8 27.5 %collective-permute-start.12 = (bf16[2,2,2,48,1536]{4,3,0,1,2:T(8,128)(2,1)S(1)}, bf16[2,2,2,48,1536]{4,3,0,1,2:T(8,128)(2,1)S(1)}, u32[]{:S(2)}, u32[]{:S(2)}) collective-permute-start(bf16[2,2,2,48,1536]{4,3,0,1,2:T(8,128)(2,1)S(1)} %bitcast.411), channel_id=1, source_target_pairs={{0,8},{2,10},{4,12},{6,14},{8,0},{10,2},{12,4},{14,6},{16,24},{18,... | collective-permute-start | bytes 3538952 | tf_op jit(solution)/shard_map/ppermute | solution.py:210
  181.1 28.4 %collective-permute-start.40 = (bf16[2,2,2,48,1536]{4,3,0,1,2:T(8,128)(2,1)S(1)}, bf16[2,2,2,48,1536]{4,3,0,1,2:T(8,128)(2,1)S(1)}, u32[]{:S(2)}, u32[]{:S(2)}) collective-permute-start(bf16[2,2,2,48,1536]{4,3,0,1,2:T(8,128)(2,1)S(1)} %bitcast.410), channel_id=1, source_target_pairs={{0,4},{2,6},{4,0},{6,2},{8,12},{10,14},{12,8},{14,10},{16,20},{18,... | collective-permute-start | bytes 3538952 | tf_op jit(solution)/shard_map/ppermute | solution.py:210
  184.2 28.1 %collective-permute-start.36 = (bf16[2,2,2,48,1536]{4,3,0,1,2:T(8,128)(2,1)S(1)}, bf16[2,2,2,48,1536]{4,3,0,1,2:T(8,128)(2,1)S(1)}, u32[]{:S(2)}, u32[]{:S(2)}) collective-permute-start(bf16[2,2,2,48,1536]{4,3,0,1,2:T(8,128)(2,1)S(1)} %bitcast.409), channel_id=1, source_target_pairs={{0,2},{2,0},{4,6},{6,4},{8,10},{10,8},{12,14},{14,12},{16,18},{18,... | collective-permute-start | bytes 3538952 | tf_op jit(solution)/shard_map/ppermute | solution.py:210
  187.3 47.8 %copy-start.20 = (bf16[2,2,2,48,1536]{4,3,0,1,2:T(8,128)(2,1)}, bf16[2,2,2,48,1536]{4,3,0,1,2:T(8,128)(2,1)S(1)}, u32[]{:S(2)}) copy-start(bf16[2,2,2,48,1536]{4,3,0,1,2:T(8,128)(2,1)S(1)} %fusion.47) | copy-start | bytes 3538948
  205.3 28.1 %collective-permute-start.32 = (bf16[2,2,2,48,1536]{4,3,0,1,2:T(8,128)(2,1)S(1)}, bf16[2,2,2,48,1536]{4,3,0,1,2:T(8,128)(2,1)S(1)}, u32[]{:S(2)}, u32[]{:S(2)}) collective-permute-start(bf16[2,2,2,48,1536]{4,3,0,1,2:T(8,128)(2,1)S(1)} %bitcast.408), channel_id=1, source_target_pairs={{0,4},{2,6},{4,0},{6,2},{8,12},{10,14},{12,8},{14,10},{16,20},{18,... | collective-permute-start | bytes 3538952 | tf_op jit(solution)/shard_map/ppermute | solution.py:210
  207.0 29.2 %copy-start.26 = (bf16[2,2,2,48,1536]{4,3,0,1,2:T(8,128)(2,1)}, bf16[2,2,2,48,1536]{4,3,0,1,2:T(8,128)(2,1)S(1)}, u32[]{:S(2)}) copy-start(bf16[2,2,2,48,1536]{4,3,0,1,2:T(8,128)(2,1)S(1)} %fusion.48) | copy-start | bytes 3538948
  209.4 30.2 %collective-permute-start.28 = (bf16[2,2,2,48,1536]{4,3,0,1,2:T(8,128)(2,1)S(1)}, bf16[2,2,2,48,1536]{4,3,0,1,2:T(8,128)(2,1)S(1)}, u32[]{:S(2)}, u32[]{:S(2)}) collective-permute-start(bf16[2,2,2,48,1536]{4,3,0,1,2:T(8,128)(2,1)S(1)} %bitcast.407), channel_id=1, source_target_pairs={{0,2},{2,0},{4,6},{6,4},{8,10},{10,8},{12,14},{14,12},{16,18},{18,... | collective-permute-start | bytes 3538952 | tf_op jit(solution)/shard_map/ppermute | solution.py:210
  212.3 125.6 %collective-permute-start.25 = (bf16[2,2,48,1536]{3,2,0,1:T(8,128)(2,1)}, bf16[2,2,48,1536]{3,2,0,1:T(8,128)(2,1)}, u32[]{:S(2)}, u32[]{:S(2)}) collective-permute-start(bf16[2,2,48,1536]{3,2,0,1:T(8,128)(2,1)} %dynamic-slice_bitcast_fusion.5), channel_id=1, source_target_pairs={{0,2},{2,0},{4,6},{6,4},{8,10},{10,8},{12,14},{14,12},{16,18},{18,... | collective-permute-start | bytes 1769480 | tf_op jit(solution)/shard_map/ppermute | solution.py:210
  233.3 106.5 %collective-permute-start.21 = (bf16[2,2,48,1536]{3,2,0,1:T(8,128)(2,1)}, bf16[2,2,48,1536]{3,2,0,1:T(8,128)(2,1)}, u32[]{:S(2)}, u32[]{:S(2)}) collective-permute-start(bf16[2,2,48,1536]{3,2,0,1:T(8,128)(2,1)} %dynamic-slice_bitcast_fusion.6), channel_id=1, source_target_pairs={{0,2},{2,0},{4,6},{6,4},{8,10},{10,8},{12,14},{14,12},{16,18},{18,... | collective-permute-start | bytes 1769480 | tf_op jit(solution)/shard_map/ppermute | solution.py:210
  239.6 102.3 %collective-permute-start.17 = (bf16[2,2,48,1536]{3,2,0,1:T(8,128)(2,1)}, bf16[2,2,48,1536]{3,2,0,1:T(8,128)(2,1)}, u32[]{:S(2)}, u32[]{:S(2)}) collective-permute-start(bf16[2,2,48,1536]{3,2,0,1:T(8,128)(2,1)} %dynamic-slice_bitcast_fusion.7), channel_id=1, source_target_pairs={{0,4},{2,6},{4,0},{6,2},{8,12},{10,14},{12,8},{14,10},{16,20},{18,... | collective-permute-start | bytes 1769480 | tf_op jit(solution)/shard_map/ppermute | solution.py:210
  242.6 102.1 %collective-permute-start.13 = (bf16[2,2,48,1536]{3,2,0,1:T(8,128)(2,1)}, bf16[2,2,48,1536]{3,2,0,1:T(8,128)(2,1)}, u32[]{:S(2)}, u32[]{:S(2)}) collective-permute-start(bf16[2,2,48,1536]{3,2,0,1:T(8,128)(2,1)} %dynamic-slice_bitcast_fusion.8), channel_id=1, source_target_pairs={{0,2},{2,0},{4,6},{6,4},{8,10},{10,8},{12,14},{14,12},{16,18},{18,... | collective-permute-start | bytes 1769480 | tf_op jit(solution)/shard_map/ppermute | solution.py:210
  244.4 101.9 %collective-permute-start.41 = (bf16[2,2,48,1536]{3,2,0,1:T(8,128)(2,1)}, bf16[2,2,48,1536]{3,2,0,1:T(8,128)(2,1)}, u32[]{:S(2)}, u32[]{:S(2)}) collective-permute-start(bf16[2,2,48,1536]{3,2,0,1:T(8,128)(2,1)} %dynamic-slice_bitcast_fusion.1), channel_id=1, source_target_pairs={{0,2},{2,0},{4,6},{6,4},{8,10},{10,8},{12,14},{14,12},{16,18},{18,... | collective-permute-start | bytes 1769480 | tf_op jit(solution)/shard_map/ppermute | solution.py:210
  254.4 60.2 %copy-start.6 = (f32[1024,768]{0,1:T(8,128)}, f32[1024,768]{0,1:T(8,128)S(1)}, u32[]{:S(2)}) copy-start(f32[1024,768]{0,1:T(8,128)S(1)} %get-tuple-element.128) | copy-start | bytes 9437188
  257.1 47.1 %copy-start.62 = (pred[128,640]{1,0:T(8,128)(4,1)S(1)}, pred[128,640]{1,0:T(8,128)(4,1)}, u32[]{:S(2)}) copy-start(pred[128,640]{1,0:T(8,128)(4,1)} %get-tuple-element.170) | copy-start | bytes 245764
  257.1 47.1 %copy-start.64 = (pred[128,640]{1,0:T(8,128)(4,1)S(1)}, pred[128,640]{1,0:T(8,128)(4,1)}, u32[]{:S(2)}) copy-start(pred[128,640]{1,0:T(8,128)(4,1)} %get-tuple-element.171) | copy-start | bytes 245764
  257.1 47.1 %copy-start.66 = (pred[128,640]{1,0:T(8,128)(4,1)S(1)}, pred[128,640]{1,0:T(8,128)(4,1)}, u32[]{:S(2)}) copy-start(pred[128,640]{1,0:T(8,128)(4,1)} %get-tuple-element.172) | copy-start | bytes 245764
  257.1 47.1 %copy-start.68 = (pred[128,640]{1,0:T(8,128)(4,1)S(1)}, pred[128,640]{1,0:T(8,128)(4,1)}, u32[]{:S(2)}) copy-start(pred[128,640]{1,0:T(8,128)(4,1)} %get-tuple-element.173) | copy-start | bytes 245764
  257.1 47.2 %copy-start.70 = (pred[128,640]{1,0:T(8,128)(4,1)S(1)}, pred[128,640]{1,0:T(8,128)(4,1)}, u32[]{:S(2)}) copy-start(pred[128,640]{1,0:T(8,128)(4,1)} %get-tuple-element.174) | copy-start | bytes 245764
  257.1 47.2 %copy-start.72 = (pred[128,640]{1,0:T(8,128)(4,1)S(1)}, pred[128,640]{1,0:T(8,128)(4,1)}, u32[]{:S(2)}) copy-start(pred[128,640]{1,0:T(8,128)(4,1)} %get-tuple-element.175) | copy-start | bytes 245764
  257.1 47.2 %copy-start.74 = (pred[128,640]{1,0:T(8,128)(4,1)S(1)}, pred[128,640]{1,0:T(8,128)(4,1)}, u32[]{:S(2)}) copy-start(pred[128,640]{1,0:T(8,128)(4,1)} %get-tuple-element.176) | copy-start | bytes 245764
  257.1 47.2 %copy-start.76 = (pred[128,640]{1,0:T(8,128)(4,1)S(1)}, pred[128,640]{1,0:T(8,128)(4,1)}, u32[]{:S(2)}) copy-start(pred[128,640]{1,0:T(8,128)(4,1)} %get-tuple-element.177) | copy-start | bytes 245764
  257.1 47.2 %copy-start.78 = (pred[128,640]{1,0:T(8,128)(4,1)S(1)}, pred[128,640]{1,0:T(8,128)(4,1)}, u32[]{:S(2)}) copy-start(pred[128,640]{1,0:T(8,128)(4,1)} %get-tuple-element.178) | copy-start | bytes 245764
  257.2 47.2 %copy-start.80 = (pred[128,640]{1,0:T(8,128)(4,1)S(1)}, pred[128,640]{1,0:T(8,128)(4,1)}, u32[]{:S(2)}) copy-start(pred[128,640]{1,0:T(8,128)(4,1)} %get-tuple-element.179) | copy-start | bytes 245764
  257.2 47.2 %copy-start.82 = (pred[128,640]{1,0:T(8,128)(4,1)S(1)}, pred[128,640]{1,0:T(8,128)(4,1)}, u32[]{:S(2)}) copy-start(pred[128,640]{1,0:T(8,128)(4,1)} %get-tuple-element.180) | copy-start | bytes 245764
  257.2 47.2 %copy-start.84 = (pred[128,640]{1,0:T(8,128)(4,1)S(1)}, pred[128,640]{1,0:T(8,128)(4,1)}, u32[]{:S(2)}) copy-start(pred[128,640]{1,0:T(8,128)(4,1)} %get-tuple-element.181) | copy-start | bytes 245764
  257.2 47.2 %copy-start.86 = (pred[128,640]{1,0:T(8,128)(4,1)S(1)}, pred[128,640]{1,0:T(8,128)(4,1)}, u32[]{:S(2)}) copy-start(pred[128,640]{1,0:T(8,128)(4,1)} %get-tuple-element.182) | copy-start | bytes 245764
  257.2 47.2 %copy-start.88 = (pred[128,640]{1,0:T(8,128)(4,1)S(1)}, pred[128,640]{1,0:T(8,128)(4,1)}, u32[]{:S(2)}) copy-start(pred[128,640]{1,0:T(8,128)(4,1)} %get-tuple-element.183) | copy-start | bytes 245764
  337.9 16.5 %collective-permute-start.37 = (bf16[2,2,48,1536]{3,2,0,1:T(8,128)(2,1)}, bf16[2,2,48,1536]{3,2,0,1:T(8,128)(2,1)S(1)}, u32[]{:S(2)}, u32[]{:S(2)}) collective-permute-start(bf16[2,2,48,1536]{3,2,0,1:T(8,128)(2,1)} %dynamic-slice_bitcast_fusion.2), channel_id=1, source_target_pairs={{0,4},{2,6},{4,0},{6,2},{8,12},{10,14},{12,8},{14,10},{16,20},{18,... | collective-permute-start | bytes 1769480 | tf_op jit(solution)/shard_map/ppermute | solution.py:210
  339.9 15.4 %collective-permute-start.33 = (bf16[2,2,48,1536]{3,2,0,1:T(8,128)(2,1)}, bf16[2,2,48,1536]{3,2,0,1:T(8,128)(2,1)S(1)}, u32[]{:S(2)}, u32[]{:S(2)}) collective-permute-start(bf16[2,2,48,1536]{3,2,0,1:T(8,128)(2,1)} %dynamic-slice_bitcast_fusion.3), channel_id=1, source_target_pairs={{0,2},{2,0},{4,6},{6,4},{8,10},{10,8},{12,14},{14,12},{16,18},{18,... | collective-permute-start | bytes 1769480 | tf_op jit(solution)/shard_map/ppermute | solution.py:210
  341.9 24.4 %collective-permute-start.29 = (bf16[2,2,48,1536]{3,2,0,1:T(8,128)(2,1)}, bf16[2,2,48,1536]{3,2,0,1:T(8,128)(2,1)S(1)}, u32[]{:S(2)}, u32[]{:S(2)}) collective-permute-start(bf16[2,2,48,1536]{3,2,0,1:T(8,128)(2,1)} %dynamic-slice_bitcast_fusion.4), channel_id=1, source_target_pairs={{0,4},{2,6},{4,0},{6,2},{8,12},{10,14},{12,8},{14,10},{16,20},{18,... | collective-permute-start | bytes 1769480 | tf_op jit(solution)/shard_map/ppermute | solution.py:210
  344.7 100.3 %collective-permute-start.3 = (bf16[1024,768]{0,1:T(8,128)(2,1)S(1)}, bf16[1024,768]{0,1:T(8,128)(2,1)S(1)}, u32[]{:S(2)}, u32[]{:S(2)}) collective-permute-start(bf16[1024,768]{0,1:T(8,128)(2,1)S(1)} %copy-done.13), channel_id=1, source_target_pairs={{0,1},{1,0},{2,3},{3,2},{4,5},{5,4},{6,7},{7,6},{8,9},{9,8},{10,11... | collective-permute-start | bytes 4718600 | tf_op jit(solution)/shard_map/ppermute | solution.py:199
  346.3 102.0 %collective-permute-start.8 = (bf16[2,2,2,48,1536]{4,3,2,1,0:T(8,128)(2,1)S(1)}, bf16[2,2,2,48,1536]{4,3,2,1,0:T(8,128)(2,1)S(1)}, u32[]{:S(2)}, u32[]{:S(2)}) collective-permute-start(bf16[2,2,2,48,1536]{4,3,2,1,0:T(8,128)(2,1)S(1)} %copy-done.34), channel_id=1, source_target_pairs={{0,2},{2,0},{4,6},{6,4},{8,10},{10,8},{12,14},{14,12},{16,18},{18,... | collective-permute-start | bytes 3538952 | tf_op jit(solution)/shard_map/ppermute | solution.py:210
  354.4 16.2 %collective-permute-start.26 = (bf16[2,48,1536]{2,1,0:T(8,128)(2,1)S(1)}, bf16[2,48,1536]{2,1,0:T(8,128)(2,1)S(1)}, u32[]{:S(2)}, u32[]{:S(2)}) collective-permute-start(bf16[2,48,1536]{2,1,0:T(8,128)(2,1)S(1)} %dynamic-slice_bitcast_fusion.14), channel_id=1, source_target_pairs={{0,4},{2,6},{4,0},{6,2},{8,12},{10,14},{12,8},{14,10},{16,20},{18,... | collective-permute-start | bytes 884744 | tf_op jit(solution)/shard_map/ppermute | solution.py:210
  355.2 16.0 %collective-permute-start.22 = (bf16[2,48,1536]{2,1,0:T(8,128)(2,1)S(1)}, bf16[2,48,1536]{2,1,0:T(8,128)(2,1)S(1)}, u32[]{:S(2)}, u32[]{:S(2)}) collective-permute-start(bf16[2,48,1536]{2,1,0:T(8,128)(2,1)S(1)} %dynamic-slice_bitcast_fusion.15), channel_id=1, source_target_pairs={{0,8},{2,10},{4,12},{6,14},{8,0},{10,2},{12,4},{14,6},{16,24},{18,... | collective-permute-start | bytes 884744 | tf_op jit(solution)/shard_map/ppermute | solution.py:210
  366.3 9.9 %collective-permute-start.18 = (bf16[2,48,1536]{2,1,0:T(8,128)(2,1)S(1)}, bf16[2,48,1536]{2,1,0:T(8,128)(2,1)S(1)}, u32[]{:S(2)}, u32[]{:S(2)}) collective-permute-start(bf16[2,48,1536]{2,1,0:T(8,128)(2,1)S(1)} %dynamic-slice_bitcast_fusion.16), channel_id=1, source_target_pairs={{0,8},{2,10},{4,12},{6,14},{8,0},{10,2},{12,4},{14,6},{16,24},{18,... | collective-permute-start | bytes 884744 | tf_op jit(solution)/shard_map/ppermute | solution.py:210
  370.6 7.0 %collective-permute-start.14 = (bf16[2,48,1536]{2,1,0:T(8,128)(2,1)S(1)}, bf16[2,48,1536]{2,1,0:T(8,128)(2,1)S(1)}, u32[]{:S(2)}, u32[]{:S(2)}) collective-permute-start(bf16[2,48,1536]{2,1,0:T(8,128)(2,1)S(1)} %dynamic-slice_bitcast_fusion.17), channel_id=1, source_target_pairs={{0,4},{2,6},{4,0},{6,2},{8,12},{10,14},{12,8},{14,10},{16,20},{18,... | collective-permute-start | bytes 884744 | tf_op jit(solution)/shard_map/ppermute | solution.py:210
  371.2 11.3 %collective-permute-start.42 = (bf16[2,48,1536]{2,1,0:T(8,128)(2,1)S(1)}, bf16[2,48,1536]{2,1,0:T(8,128)(2,1)S(1)}, u32[]{:S(2)}, u32[]{:S(2)}) collective-permute-start(bf16[2,48,1536]{2,1,0:T(8,128)(2,1)S(1)} %dynamic-slice_bitcast_fusion.10), channel_id=1, source_target_pairs={{0,8},{2,10},{4,12},{6,14},{8,0},{10,2},{12,4},{14,6},{16,24},{18,... | collective-permute-start | bytes 884744 | tf_op jit(solution)/shard_map/ppermute | solution.py:210
  376.2 14.2 %collective-permute-start.38 = (bf16[2,48,1536]{2,1,0:T(8,128)(2,1)S(1)}, bf16[2,48,1536]{2,1,0:T(8,128)(2,1)S(1)}, u32[]{:S(2)}, u32[]{:S(2)}) collective-permute-start(bf16[2,48,1536]{2,1,0:T(8,128)(2,1)S(1)} %dynamic-slice_bitcast_fusion.11), channel_id=1, source_target_pairs={{0,8},{2,10},{4,12},{6,14},{8,0},{10,2},{12,4},{14,6},{16,24},{18,... | collective-permute-start | bytes 884744 | tf_op jit(solution)/shard_map/ppermute | solution.py:210
  377.7 21.1 %collective-permute-start.34 = (bf16[2,48,1536]{2,1,0:T(8,128)(2,1)S(1)}, bf16[2,48,1536]{2,1,0:T(8,128)(2,1)S(1)}, u32[]{:S(2)}, u32[]{:S(2)}) collective-permute-start(bf16[2,48,1536]{2,1,0:T(8,128)(2,1)S(1)} %dynamic-slice_bitcast_fusion.12), channel_id=1, source_target_pairs={{0,8},{2,10},{4,12},{6,14},{8,0},{10,2},{12,4},{14,6},{16,24},{18,... | collective-permute-start | bytes 884744 | tf_op jit(solution)/shard_map/ppermute | solution.py:210
  382.5 20.8 %collective-permute-start.30 = (bf16[2,48,1536]{2,1,0:T(8,128)(2,1)S(1)}, bf16[2,48,1536]{2,1,0:T(8,128)(2,1)S(1)}, u32[]{:S(2)}, u32[]{:S(2)}) collective-permute-start(bf16[2,48,1536]{2,1,0:T(8,128)(2,1)S(1)} %dynamic-slice_bitcast_fusion.13), channel_id=1, source_target_pairs={{0,8},{2,10},{4,12},{6,14},{8,0},{10,2},{12,4},{14,6},{16,24},{18,... | collective-permute-start | bytes 884744 | tf_op jit(solution)/shard_map/ppermute | solution.py:210
  390.4 13.5 %collective-permute-start.27 = (bf16[48,1536]{1,0:T(8,128)(2,1)S(1)}, bf16[48,1536]{1,0:T(8,128)(2,1)S(1)}, u32[]{:S(2)}, u32[]{:S(2)}) collective-permute-start(bf16[48,1536]{1,0:T(8,128)(2,1)S(1)} %dynamic-slice_bitcast_fusion.23), channel_id=1, source_target_pairs={{0,16},{2,18},{4,20},{6,22},{8,24},{10,26},{12,28},{14,30},{16,0},... | collective-permute-start | bytes 442376 | tf_op jit(solution)/shard_map/ppermute | solution.py:210
  398.8 18.0 %collective-permute-start.23 = (bf16[48,1536]{1,0:T(8,128)(2,1)S(1)}, bf16[48,1536]{1,0:T(8,128)(2,1)S(1)}, u32[]{:S(2)}, u32[]{:S(2)}) collective-permute-start(bf16[48,1536]{1,0:T(8,128)(2,1)S(1)} %dynamic-slice_bitcast_fusion.24), channel_id=1, source_target_pairs={{0,16},{2,18},{4,20},{6,22},{8,24},{10,26},{12,28},{14,30},{16,0},... | collective-permute-start | bytes 442376 | tf_op jit(solution)/shard_map/ppermute | solution.py:210
  403.3 19.8 %collective-permute-start.19 = (bf16[48,1536]{1,0:T(8,128)(2,1)S(1)}, bf16[48,1536]{1,0:T(8,128)(2,1)S(1)}, u32[]{:S(2)}, u32[]{:S(2)}) collective-permute-start(bf16[48,1536]{1,0:T(8,128)(2,1)S(1)} %dynamic-slice_bitcast_fusion.25), channel_id=1, source_target_pairs={{0,16},{2,18},{4,20},{6,22},{8,24},{10,26},{12,28},{14,30},{16,0},... | collective-permute-start | bytes 442376 | tf_op jit(solution)/shard_map/ppermute | solution.py:210
  404.0 22.3 %collective-permute-start.15 = (bf16[48,1536]{1,0:T(8,128)(2,1)S(1)}, bf16[48,1536]{1,0:T(8,128)(2,1)S(1)}, u32[]{:S(2)}, u32[]{:S(2)}) collective-permute-start(bf16[48,1536]{1,0:T(8,128)(2,1)S(1)} %dynamic-slice_bitcast_fusion.26), channel_id=1, source_target_pairs={{0,16},{2,18},{4,20},{6,22},{8,24},{10,26},{12,28},{14,30},{16,0},... | collective-permute-start | bytes 442376 | tf_op jit(solution)/shard_map/ppermute | solution.py:210
  416.8 15.8 %collective-permute-start.43 = (bf16[48,1536]{1,0:T(8,128)(2,1)S(1)}, bf16[48,1536]{1,0:T(8,128)(2,1)S(1)}, u32[]{:S(2)}, u32[]{:S(2)}) collective-permute-start(bf16[48,1536]{1,0:T(8,128)(2,1)S(1)} %dynamic-slice_bitcast_fusion.19), channel_id=1, source_target_pairs={{0,16},{2,18},{4,20},{6,22},{8,24},{10,26},{12,28},{14,30},{16,0},... | collective-permute-start | bytes 442376 | tf_op jit(solution)/shard_map/ppermute | solution.py:210
  423.1 17.4 %collective-permute-start.39 = (bf16[48,1536]{1,0:T(8,128)(2,1)S(1)}, bf16[48,1536]{1,0:T(8,128)(2,1)S(1)}, u32[]{:S(2)}, u32[]{:S(2)}) collective-permute-start(bf16[48,1536]{1,0:T(8,128)(2,1)S(1)} %dynamic-slice_bitcast_fusion.20), channel_id=1, source_target_pairs={{0,16},{2,18},{4,20},{6,22},{8,24},{10,26},{12,28},{14,30},{16,0},... | collective-permute-start | bytes 442376 | tf_op jit(solution)/shard_map/ppermute | solution.py:210
  426.3 16.0 %collective-permute-start.35 = (bf16[48,1536]{1,0:T(8,128)(2,1)S(1)}, bf16[48,1536]{1,0:T(8,128)(2,1)S(1)}, u32[]{:S(2)}, u32[]{:S(2)}) collective-permute-start(bf16[48,1536]{1,0:T(8,128)(2,1)S(1)} %dynamic-slice_bitcast_fusion.21), channel_id=1, source_target_pairs={{0,16},{2,18},{4,20},{6,22},{8,24},{10,26},{12,28},{14,30},{16,0},... | collective-permute-start | bytes 442376 | tf_op jit(solution)/shard_map/ppermute | solution.py:210
  432.6 11.2 %collective-permute-start.31 = (bf16[48,1536]{1,0:T(8,128)(2,1)S(1)}, bf16[48,1536]{1,0:T(8,128)(2,1)S(1)}, u32[]{:S(2)}, u32[]{:S(2)}) collective-permute-start(bf16[48,1536]{1,0:T(8,128)(2,1)S(1)} %dynamic-slice_bitcast_fusion.22), channel_id=1, source_target_pairs={{0,16},{2,18},{4,20},{6,22},{8,24},{10,26},{12,28},{14,30},{16,0},... | collective-permute-start | bytes 442376 | tf_op jit(solution)/shard_map/ppermute | solution.py:210
  446.4 3.8 collective-permute-start.4
  450.3 4.8 collective-permute-start.5
  453.9 12.7 %collective-permute-start.9 = (bf16[2,2,48,1536]{3,2,1,0:T(8,128)(2,1)}, bf16[2,2,48,1536]{3,2,1,0:T(8,128)(2,1)}, u32[]{:S(2)}, u32[]{:S(2)}) collective-permute-start(bf16[2,2,48,1536]{3,2,1,0:T(8,128)(2,1)} %dynamic-slice_bitcast_fusion.9), channel_id=1, source_target_pairs={{0,4},{2,6},{4,0},{6,2},{8,12},{10,14},{12,8},{14,10},{16,20},{18,... | collective-permute-start | bytes 1769480 | tf_op jit(solution)/shard_map/ppermute | solution.py:210
  455.1 3.8 collective-permute-start.6
  458.9 7.0 %collective-permute-start.7 = (f32[4800]{0:T(1024)S(1)}, f32[4800]{0:T(1024)S(1)}, u32[]{:S(2)}, u32[]{:S(2)}) collective-permute-start(f32[4800]{0:T(1024)S(1)} %add.1921), channel_id=1, source_target_pairs={{0,16},{2,18},{4,20},{6,22},{8,24},{10,26},{12,28},{14,30},{16,0},... | collective-permute-start | bytes 57608 | tf_op jit(solution)/shard_map/ppermute | solution.py:210
  467.9 8.1 %collective-permute-start.10 = (bf16[2,48,1536]{2,1,0:T(8,128)(2,1)S(1)}, bf16[2,48,1536]{2,1,0:T(8,128)(2,1)S(1)}, u32[]{:S(2)}, u32[]{:S(2)}) collective-permute-start(bf16[2,48,1536]{2,1,0:T(8,128)(2,1)S(1)} %dynamic-slice_bitcast_fusion.18), channel_id=1, source_target_pairs={{0,8},{2,10},{4,12},{6,14},{8,0},{10,2},{12,4},{14,6},{16,24},{18,... | collective-permute-start | bytes 884744 | tf_op jit(solution)/shard_map/ppermute | solution.py:210
  476.1 7.7 %collective-permute-start.11 = (bf16[48,1536]{1,0:T(8,128)(2,1)S(1)}, bf16[48,1536]{1,0:T(8,128)(2,1)S(1)}, u32[]{:S(2)}, u32[]{:S(2)}) collective-permute-start(bf16[48,1536]{1,0:T(8,128)(2,1)S(1)} %dynamic-slice_bitcast_fusion.27), channel_id=1, source_target_pairs={{0,16},{2,18},{4,20},{6,22},{8,24},{10,26},{12,28},{14,30},{16,0},... | collective-permute-start | bytes 442376 | tf_op jit(solution)/shard_map/ppermute | solution.py:210
  (109 other events, 591.1 us)

commit v2 on v1

v2 whole, which is shorter than its diff:
```python
import functools

import jax
import jax.numpy as jnp
from jax import lax
from jax.experimental import pallas as pl
from jax.experimental.pallas import tpu as pltpu
from jax.sharding import PartitionSpec as P

HEAD_DIM = 64
CAP = 320
EPS = 1e-06
NEG = -1e30
HIGH = lax.Precision.HIGHEST
BLOCK = 128
SPAN = 6 * BLOCK
LIMIT = 48 * 1024 * 1024
F32 = jnp.float32
BF16 = jnp.bfloat16


def offset_bucket():
    lane = jnp.arange(SPAN, dtype=jnp.int32)
    offset = jnp.where(lane < 5 * BLOCK, lane, lane - SPAN) - 2 * BLOCK
    distance = jnp.abs(offset)
    coarse = jnp.full_like(distance, 8)
    for limit in (12, 16, 23, 32, 46, 64, 91):
        coarse = coarse + (distance >= limit).astype(jnp.int32)
    bucket = jnp.where(distance < 8, distance, coarse)
    return bucket + 16 * (offset > 0).astype(jnp.int32)


def offset_bias(table, bucket):
    result = jnp.zeros((table.shape[1], SPAN), F32)
    for index in range(table.shape[0]):
        result = jnp.where(bucket[None] == index, table[index][:, None], result)
    return result.reshape(-1, 2, SPAN)


def offset_table_grad(sums, bucket, count):
    flat = sums.reshape(-1, SPAN)
    same = bucket[None, :] == jnp.arange(count, dtype=jnp.int32)[:, None]
    return jnp.sum(jnp.where(same[:, None, :], flat[None], 0.0), axis=-1)


def tile_ranges(segment):
    rows = segment.reshape(-1, BLOCK)
    first = jnp.sum((segment[None] < rows[:, :1]).astype(jnp.int32), axis=1) // BLOCK
    end = (jnp.sum((segment[None] <= rows[:, -1:]).astype(jnp.int32), axis=1) + BLOCK - 1) // BLOCK
    return jnp.concatenate([first, end])


def row_norm(values, gain):
    inverse = lax.rsqrt(jnp.mean(values * values, axis=-1, keepdims=True) + EPS)
    return (values * inverse * gain, inverse)


def norm_back(grad_out, values, inverse, gain):
    scaled = grad_out * gain
    grad_gain = jnp.sum(grad_out * values * inverse, axis=0)
    grad_in = inverse * scaled - values * inverse**3 * jnp.mean(
        scaled * values, axis=-1, keepdims=True
    )
    return (grad_in, grad_gain)


def dot_t(left, right):
    return lax.dot_general(left, right, (((1,), (1,)), ((), ())), preferred_element_type=F32)


def dot_n(left, right):
    return lax.dot_general(left, right, (((1,), (0,)), ((), ())), preferred_element_type=F32)


def t_dot(left, right):
    return lax.dot_general(left, right, (((0,), (0,)), ((), ())), preferred_element_type=F32)


def skew_rows(vector):
    made = jnp.broadcast_to(vector, (8, SPAN))
    row = lax.broadcasted_iota(jnp.int32, (8, SPAN), 0)
    for step in (1, 2, 4):
        made = jnp.where((row & step) != 0, pltpu.roll(made, step, 1), made)
    for step in (8, 16, 32, 64):
        made = jnp.concatenate([made, pltpu.roll(made, step, 1)], axis=0)
    return made


def unskew_sum(band):
    held = jnp.concatenate([band, jnp.zeros((BLOCK, SPAN - band.shape[1]), F32)], axis=1)
    for step in (64, 32, 16, 8):
        held = held[:step] + pltpu.roll(held[step:], SPAN - step, 1)
    row = lax.broadcasted_iota(jnp.int32, (8, SPAN), 0)
    for step in (1, 2, 4):
        held = jnp.where((row & step) != 0, pltpu.roll(held, SPAN - step, 1), held)
    return jnp.sum(held, axis=0, keepdims=True)


def band_lanes(tile, place):
    start = (jnp.clip(tile - place, -2, 2) + 2) * BLOCK
    return pl.ds(pl.multiple_of(start, BLOCK), BLOCK)


def lane_half(array, head):
    lane = lax.broadcasted_iota(jnp.int32, array.shape, 1)
    return jnp.where((lane >= HEAD_DIM) == (head == 1), array, jnp.zeros_like(array))


def over_windows(range_ref, place, tiles, step):
    first, end = range_ref[place], range_ref[tiles + place]
    need = end - first
    sizes = sorted({min(3, tiles), min(5, tiles), tiles})
    below = 0
    for size in sizes:

        @pl.when((need > below) & (need <= size))
        def _(size=size):
            step(jnp.minimum(first, tiles - size), size)

        below = size


def window_scores(query_h, keys, same, bias_ref, head, place, start, size):
    raw = dot_t(query_h, keys)
    bias = jnp.concatenate(
        [bias_ref[head, :, band_lanes(start + tile, place)] for tile in range(size)], axis=1
    )
    return jnp.where(same, raw + bias, NEG)


def attend_kernel(range_ref, q_ref, k_ref, v_ref, vec_ref, seg_col_ref, seg_row_ref, out_ref, bias_ref):
    place = pl.program_id(1)
    tiles = k_ref.shape[1] // BLOCK

    @pl.when(place == 0)
    def _():
        for head in range(2):
            bias_ref[head] = skew_rows(vec_ref[0, head : head + 1, :])[:, : 5 * BLOCK]

    def step(start, size):
        window = pl.ds(pl.multiple_of(start * BLOCK, BLOCK), size * BLOCK)
        query = q_ref[0] * jnp.asarray(HEAD_DIM**-0.5, BF16)
        keys, values = k_ref[0, window, :], v_ref[0, window, :]
        same = seg_col_ref[...] == seg_row_ref[:, window]
        total = None
        for head in range(2):
            scores = window_scores(
                lane_half(query, head), keys, same, bias_ref, head, place, start, size
            )
            expo = jnp.exp(scores - jnp.max(scores, axis=-1, keepdims=True))
            inverse = 1.0 / jnp.sum(expo, axis=-1, keepdims=True)
            mixed = lane_half(dot_n(expo.astype(BF16), values) * inverse, head)
            total = mixed if total is None else total + mixed
        out_ref[...] = total.astype(BF16)

    over_windows(range_ref, place, tiles, step)


def attend_back_kernel(
    range_ref,
    q_ref,
    k_ref,
    v_ref,
    vec_ref,
    seg_col_ref,
    seg_row_ref,
    grad_ref,
    out_ref,
    sums_ref,
    bias_ref,
    band_ref,
    dk_ref,
    dv_ref,
):
    place = pl.program_id(1)
    tiles = k_ref.shape[1] // BLOCK

    @pl.when(place == 0)
    def _():
        dk_ref[...] = jnp.zeros_like(dk_ref)
        dv_ref[...] = jnp.zeros_like(dv_ref)
        band_ref[...] = jnp.zeros_like(band_ref)
        for head in range(2):
            bias_ref[head] = skew_rows(vec_ref[0, head : head + 1, :])[:, : 5 * BLOCK]

    rows = pl.ds(pl.multiple_of(place * BLOCK, BLOCK), BLOCK)

    def step(start, size):
        window = pl.ds(pl.multiple_of(start * BLOCK, BLOCK), size * BLOCK)
        query = q_ref[0] * jnp.asarray(HEAD_DIM**-0.5, BF16)
        keys, values, grad = k_ref[0, window, :], v_ref[0, window, :], grad_ref[...]
        same = seg_col_ref[...] == seg_row_ref[:, window]
        dq = None
        for head in range(2):
            query_h, grad_h = lane_half(query, head), lane_half(grad, head)
            scores = window_scores(query_h, keys, same, bias_ref, head, place, start, size)
            expo = jnp.exp(scores - jnp.max(scores, axis=-1, keepdims=True))
            probs = expo * (1.0 / jnp.sum(expo, axis=-1, keepdims=True))
            grad_probs = dot_t(grad_h, values)
            inner = jnp.sum(grad_probs * probs, axis=-1, keepdims=True)
            grad_scores = probs * (grad_probs - inner)
            for tile in range(size):
                band_ref[head, :, band_lanes(start + tile, place)] += grad_scores[
                    :, tile * BLOCK : (tile + 1) * BLOCK
                ]
            low = grad_scores.astype(BF16)
            dv_ref[window, :] += t_dot(probs.astype(BF16), grad_h)
            dk_ref[window, :] += t_dot(low, query_h)
            part = lane_half(dot_n(low, keys), head)
            dq = part if dq is None else dq + part
        out_ref[0, rows, :] = (dq * HEAD_DIM**-0.5).astype(BF16)

    over_windows(range_ref, place, tiles, step)

    @pl.when(place == tiles - 1)
    def _():
        out_ref[1] = dk_ref[...].astype(BF16)
        out_ref[2] = dv_ref[...].astype(BF16)
        for head in range(2):
            sums_ref[0, head : head + 1, :] = unskew_sum(band_ref[head])


def attention_specs(length):
    return [
        pl.BlockSpec((1, BLOCK, BLOCK), lambda p, i, r: (0, i, p)),
        pl.BlockSpec((1, length, BLOCK), lambda p, i, r: (1, 0, p)),
        pl.BlockSpec((1, length, BLOCK), lambda p, i, r: (2, 0, p)),
        pl.BlockSpec((1, 2, SPAN), lambda p, i, r: (p, 0, 0)),
        pl.BlockSpec((BLOCK, 1), lambda p, i, r: (i, 0)),
        pl.BlockSpec((1, length), lambda p, i, r: (0, 0)),
    ]


def attend(projected, bias, segment):
    _, length, width = projected.shape
    pairs = width // BLOCK
    return pl.pallas_call(
        attend_kernel,
        grid_spec=pltpu.PrefetchScalarGridSpec(
            num_scalar_prefetch=1,
            grid=(pairs, length // BLOCK),
            in_specs=attention_specs(length),
            out_specs=pl.BlockSpec((BLOCK, BLOCK), lambda p, i, r: (i, p)),
            scratch_shapes=[pltpu.VMEM((2, BLOCK, 5 * BLOCK), F32)],
        ),
        out_shape=jax.ShapeDtypeStruct((length, width), BF16),
        compiler_params=pltpu.CompilerParams(vmem_limit_bytes=LIMIT),
        cost_estimate=pl.CostEstimate(
            flops=16 * length * length * width, bytes_accessed=8 * length * width, transcendentals=6 * length * length
        ),
    )(tile_ranges(segment), projected, projected, projected, bias, segment[:, None], segment[None, :])


def attend_back(projected, bias, segment, grad):
    _, length, width = projected.shape
    pairs = width // BLOCK
    return pl.pallas_call(
        attend_back_kernel,
        grid_spec=pltpu.PrefetchScalarGridSpec(
            num_scalar_prefetch=1,
            grid=(pairs, length // BLOCK),
            in_specs=attention_specs(length) + [pl.BlockSpec((BLOCK, BLOCK), lambda p, i, r: (i, p))],
            out_specs=[
                pl.BlockSpec((3, length, BLOCK), lambda p, i, r: (0, 0, p)),
                pl.BlockSpec((1, 2, SPAN), lambda p, i, r: (p, 0, 0)),
            ],
            scratch_shapes=[
                pltpu.VMEM((2, BLOCK, 5 * BLOCK), F32),
                pltpu.VMEM((2, BLOCK, 5 * BLOCK), F32),
                pltpu.VMEM((length, BLOCK), F32),
                pltpu.VMEM((length, BLOCK), F32),
            ],
        ),
        out_shape=[
            jax.ShapeDtypeStruct((3, length, width), BF16),
            jax.ShapeDtypeStruct((pairs, 2, SPAN), F32),
        ],
        compiler_params=pltpu.CompilerParams(vmem_limit_bytes=LIMIT),
        cost_estimate=pl.CostEstimate(
            flops=48 * length * length * width, bytes_accessed=16 * length * width, transcendentals=6 * length * length
        ),
    )(tile_ranges(segment), projected, projected, projected, bias, segment[:, None], segment[None, :], grad)


def pair_sum(part, size):
    if size != 2:
        return lax.psum(part.astype(F32), "tensor")
    other = lax.ppermute(part, "tensor", [(0, 1), (1, 0)])
    return part.astype(F32) + other.astype(F32)


def bits_of(size):
    bits = size.bit_length() - 1
    assert 1 << bits == size
    return bits


def swap(array, size, bit):
    return lax.ppermute(array, "dp", [(i, i ^ (1 << bit)) for i in range(size)])


def scatter_sum(unit, size, order):
    bits = bits_of(size)
    parts, rows, columns = unit.shape
    me = lax.axis_index("dp")
    held = unit.reshape((parts,) + (2,) * bits + (rows // size, columns))
    left = list(range(bits - 1, -1, -1))
    for step, bit in enumerate(order):
        axis = 1 + left.index(bit)
        mine = (me >> bit) & 1
        sent = lax.dynamic_index_in_dim(held, 1 - mine, axis, keepdims=False)
        kept = lax.dynamic_index_in_dim(held, mine, axis, keepdims=False)
        got = swap(sent, size, bit)
        held = kept.astype(F32) + got.astype(F32)
        if step < bits - 1:
            held = held.astype(BF16)
        left.remove(bit)
    return held


def small_sum(array, size):
    for bit in range(bits_of(size)):
        array = array + swap(array, size, bit)
    return array


def orders_of(size):
    bits = bits_of(size)
    if bits == 4:
        return [(0, 1, 2, 3), (1, 0, 2, 3)]
    return [tuple(range(bits)), tuple(range(bits - 1, -1, -1))]


def halves_sum(left, right, size):
    one, other = orders_of(size)
    return jnp.concatenate([scatter_sum(left, size, one), scatter_sum(right, size, other)], axis=0)


def body(
    dp,
    tp,
    tokens,
    gain_attn,
    query_key_value_weight,
    attn_out_weight,
    position_bias_matrix,
    gain_expert,
    router,
    expert_in,
    expert_out,
    segments,
    routes,
    slots,
    cotangent,
):
    seqs, length, width = tokens.shape
    count = seqs * length
    experts = expert_in.shape[0]
    places = experts * CAP
    local = attn_out_weight.shape[0]
    half = experts // 2
    inputs = tokens.astype(F32).reshape(count, width)
    normed_a, inverse_a = row_norm(inputs, gain_attn)
    act_a = normed_a.astype(BF16)
    projected = jnp.einsum(
        "td,cde->cte", act_a, query_key_value_weight, preferred_element_type=F32
    ).astype(BF16)
    bucket = offset_bucket()
    bias = offset_bias(position_bias_matrix, bucket)
    per_seq = projected.reshape(3, seqs, length, local)
    flat_att = jnp.concatenate([attend(per_seq[:, s], bias, segments[s]) for s in range(seqs)], axis=0)
    attn_part = jnp.dot(flat_att, attn_out_weight, preferred_element_type=F32).astype(BF16)
    hidden_res = inputs + pair_sum(attn_part, tp)
    normed_e, inverse_e = row_norm(hidden_res, gain_expert)
    logits = jnp.dot(normed_e, router, precision=HIGH, preferred_element_type=F32)
    chance = jax.nn.softmax(logits, axis=-1)
    route_flat = routes.reshape(count)
    onehot = (route_flat[:, None] == jnp.arange(experts, dtype=jnp.int32)[None, :]).astype(F32)
    gate = jnp.sum(chance * onehot, axis=-1)
    block = jnp.arange(count, dtype=jnp.int32) // length
    place = (block * places) + route_flat * CAP + slots.reshape(count)
    spot = jnp.arange(seqs * places, dtype=jnp.int32)
    to_slot = (spot[:, None] == place[None, :]).astype(BF16)
    to_token = (place[:, None] == spot[None, :]).astype(BF16)
    act_e = normed_e.astype(BF16)
    upstream = cotangent.astype(F32).reshape(count, width)
    scaled_up = (upstream * gate[:, None]).astype(BF16)

    def dispatch(array):
        made = jnp.dot(to_slot, array, preferred_element_type=F32).astype(BF16)
        made = made.reshape(seqs, experts, CAP, width)
        return jnp.transpose(made, (1, 0, 2, 3)).reshape(experts, seqs * CAP, width)

    def collect(array):
        array = jnp.transpose(array.reshape(experts, seqs, CAP, width), (1, 0, 2, 3))
        array = array.reshape(seqs * places, width)
        return jnp.dot(to_token, array, preferred_element_type=F32).astype(BF16)

    dispatched = dispatch(act_e)
    slot_grad = dispatch(scaled_up)
    inner = jnp.einsum("ecd,edf->ecf", dispatched, expert_in, preferred_element_type=F32)
    activated = jax.nn.gelu(inner).astype(BF16)
    pieces = (slice(0, half), slice(half, experts))
    grad_out_t = [
        jnp.einsum("ecd,ecf->edf", slot_grad[p], activated[p], preferred_element_type=F32).astype(BF16)
        for p in pieces
    ]
    grad_out_t, slot_grad = lax.optimization_barrier((grad_out_t, slot_grad))
    summed_out = halves_sum(*grad_out_t, dp)
    grad_act = jnp.einsum("ecd,efd->ecf", slot_grad, expert_out, preferred_element_type=F32)
    unused, gelu_pull = jax.vjp(jax.nn.gelu, inner)
    grad_inner = gelu_pull(grad_act)[0].astype(BF16)
    grad_in = [
        jnp.einsum("ecd,ecf->edf", dispatched[p], grad_inner[p], preferred_element_type=F32).astype(BF16)
        for p in pieces
    ]
    grad_in, activated, grad_inner = lax.optimization_barrier((grad_in, activated, grad_inner))
    summed_in = halves_sum(*grad_in, dp)
    returned = jnp.einsum("ecf,efd->ecd", activated, expert_out, preferred_element_type=F32).astype(BF16)
    expert_total = pair_sum(collect(returned), tp)
    grad_disp = jnp.einsum("ecf,edf->ecd", grad_inner, expert_in, preferred_element_type=F32).astype(BF16)
    back_expert = pair_sum(collect(grad_disp), tp)
    output = (hidden_res + expert_total * gate[:, None]).astype(BF16).reshape(seqs, length, width)
    grad_gate = jnp.sum(upstream * expert_total, axis=-1)
    grad_logits = (grad_gate * gate)[:, None] * (onehot - chance)
    grad_router = jnp.dot(normed_e.T, grad_logits, precision=HIGH, preferred_element_type=F32)
    grad_normed_e = back_expert + jnp.dot(
        grad_logits, router.T, precision=HIGH, preferred_element_type=F32
    )
    grad_hidden_part, grad_gain_expert = norm_back(grad_normed_e, hidden_res, inverse_e, gain_expert)
    grad_hidden = upstream + grad_hidden_part
    grad_hidden_low = grad_hidden.astype(BF16)
    grad_attn_out_t = jnp.dot(grad_hidden_low.T, flat_att, preferred_element_type=F32).astype(BF16)
    grad_attended = jnp.dot(
        grad_hidden_low, attn_out_weight.T, preferred_element_type=F32
    ).astype(BF16)
    parts, bands = [], None
    for s in range(seqs):
        part, band = attend_back(
            per_seq[:, s], bias, segments[s], grad_attended.reshape(seqs, length, local)[s]
        )
        parts.append(part)
        bands = band if bands is None else bands + band
    grads = jnp.concatenate(parts, axis=1)
    weight_grads = [
        jnp.dot(act_a.T, grads[k], preferred_element_type=F32).astype(BF16) for k in range(3)
    ]
    last = halves_sum(jnp.stack(weight_grads[:2]), jnp.stack([weight_grads[2], grad_attn_out_t]), dp)
    grad_act_a = jnp.einsum("cte,cde->td", grads, query_key_value_weight, preferred_element_type=F32)
    grad_table = offset_table_grad(bands, bucket, position_bias_matrix.shape[0])
    back_attn = pair_sum(grad_act_a.astype(BF16), tp)
    grad_in_part, grad_gain_attn = norm_back(back_attn, inputs, inverse_a, gain_attn)
    grad_tokens = (grad_hidden + grad_in_part).reshape(seqs, length, width)
    small = jnp.concatenate(
        [grad_gain_attn, grad_gain_expert, grad_router.T.reshape(-1), grad_table.reshape(-1)]
    )
    small = small_sum(small, dp)
    me = lax.axis_index("dp")
    share = width // dp
    wide = lax.dynamic_slice_in_dim(small[: 6 * width].reshape(6, width), me * share, share, axis=1)
    return (
        output,
        grad_tokens,
        wide[0],
        last[:3],
        last[3].T,
        small[6 * width :].reshape(position_bias_matrix.shape),
        wide[1],
        wide[2:].T,
        summed_in,
        jnp.transpose(summed_out, (0, 2, 1)),
    )


def solution(mesh):
    in_specs = (
        P("dp", None, None),
        P(),
        P(None, None, "tensor"),
        P("tensor", None),
        P(None, "tensor"),
        P(),
        P(),
        P(None, None, "tensor"),
        P(None, "tensor", None),
        P("dp", None),
        P("dp", None),
        P("dp", None),
        P("dp", None, None),
    )
    out_specs = (
        P("dp", None, None),
        P("dp", None, None),
        P("dp"),
        P(None, "dp", "tensor"),
        P("tensor", "dp"),
        P(None, "tensor"),
        P("dp"),
        P("dp", None),
        P(None, "dp", "tensor"),
        P(None, "tensor", "dp"),
    )
    run = functools.partial(body, mesh.shape["dp"], mesh.shape["tensor"])
    return jax.shard_map(run, mesh=mesh, in_specs=in_specs, out_specs=out_specs, check_vma=False)
```

time: 490 us -> 471 us (0.961)
  waiting for transfers between devices: 150 us -> 172 us
  other arithmetic: 66.1 us -> 46.6 us
  Pallas kernels: 74.1 us -> 62.4 us
  starting transfers between devices: 51 us -> 40.8 us
  matrix products: 99.9 us -> 91.1 us
  local copies, waits for them, and re-layouts: 41.5 us -> 49 us
    ppermute x40 -> x28, waiting for transfers between devices: 149 us -> 172 us  [swap(): return lax.ppermute(array, 'dp', [(i, i ^ 1 << bit) for i in range(size)])]
    select_n x1 -> x2, other arithmetic: 19.3 us -> 0.33 us  [the longest x1 0.32 us: offset_bias(): result = jnp.where(bucket[None] == index, table[index][:, None], result)]
    pallas_call x2, Pallas kernels: 74.1 us -> 62.4 us  [the longest x1 40.2 us: attend_back(): pl.pallas_call(attend_back_kernel, grid_spec=pltpu.PrefetchScalarGridSpec...]
    ppermute x40 -> x28, starting transfers between devices: 49.9 us -> 39.7 us  [swap(): return lax.ppermute(array, 'dp', [(i, i ^ 1 << bit) for i in range(size)])]
    reduce_sum x2, other arithmetic: 10.2 us -> 1.08 us  [the longest x1 0.96 us: tile_ranges(): jnp.sum((segment[None] < rows[:, :1]).astype(jnp.int32), axis=1) // BLOCK]
    dot_general x1, matrix products: 14.2 us -> 6.68 us  [body(): jnp.einsum('ecd,edf->ecf', dispatched, expert_in, preferred_element_type=...]
    dynamic_slice x5 -> x4, local copies, waits for them, and re-layouts: 1.42 us -> 7.53 us  [scatter_sum(): kept = lax.dynamic_index_in_dim(held, mine, axis, keepdims=False)]
    dot_general x8 -> x4, matrix products: 18.5 us -> 22.9 us  [the longest x2 12.1 us: body(): jnp.einsum('ecd,ecf->edf', dispatched[p], grad_inner[p], preferred_elemen...]
  transfers between devices with their start and end apart: 44 -> 32, of which waited for: 26 -> 18; matrix products, arithmetic and copies ran while one was open for 19% -> 21% of each run, Pallas kernels for 10% -> 9%
where the time goes in v2:
time: 471 us; the launch traced here: 464 us
  waiting for transfers between devices  172 us (37%)
  matrix products  91.1 us (19%)
  Pallas kernels  62.4 us (13%)
  local copies, waits for them, and re-layouts  49 us (10%)
  other arithmetic  46.6 us (10%)
  starting transfers between devices  40.8 us (9%)
    ppermute x28, waiting for transfers between devices, swap(): return lax.ppermute(array, 'dp', [(i, i ^ 1 << bit) for i in range(size)])  172 us
    pallas_call x1, Pallas kernels, attend_back(): pl.pallas_call(attend_back_kernel, grid_spec=pltpu.PrefetchScalarGridSpec...  40.2 us
    ppermute x28, starting transfers between devices, swap(): return lax.ppermute(array, 'dp', [(i, i ^ 1 << bit) for i in range(size)])  39.7 us
    pallas_call x1, Pallas kernels, attend(): pl.pallas_call(attend_kernel, grid_spec=pltpu.PrefetchScalarGridSpec(num_...  22.2 us
    unnamed x145, local copies, waits for them, and re-layouts  19.3 us
    convert_element_type x18, other arithmetic, scatter_sum(): held = held.astype(BF16)  18.7 us
    dot_general x1, matrix products, body(): jnp.einsum('ecd,efd->ecf', slot_grad, expert_out, preferred_element_type=...  14.4 us
    dot_general x2, matrix products, body(): jnp.einsum('ecd,ecf->edf', dispatched[p], grad_inner[p], preferred_elemen...  12.1 us
  transfers between devices with their start and end apart: 32, of which 18 were waited for; matrix products, arithmetic and copies ran while one was open for 21% of the time, Pallas kernels for 9%

profile of v2, /device:TPU:0, one launch (start us, length us, event | category | flops | bytes accessed | tf_op | source)
XLA Modules:
  0.0 464.0 jit_solution(5428821578024973170)
XLA Ops:
  7.2 2.3 slice_reduce_fusion.31
  19.1 3.8 convert_bitcast_fusion.1.q_ref.k_ref.v_ref
  23.4 22.2 %shard_map.204 = bf16[1024,384]{1,0:T(8,128)(2,1)S(1)} custom-call(s32[16]{0:T(128)S(1)} %pad_add_fusion.range_ref, bf16[3,1024,384]{2,1,0:T(8,128)(2,1)S(1)} %convert_bitcast_fusion.1.q_ref.k_ref.v_ref, bf16[3,1024,384]{2,1,0:T(8,128)(2,1)S(1)} %convert_bitcast_fusion.1.q_ref.k_ref.v_ref, bf16[3,1024,384]{2,1,0:T(8,128)(2,1)S(1)} %convert_bitcast_fusion.1.q_ref.k_ref.v_ref, ...), custom_call_target="tpu_custom_call" | custom-call | flops 6442450944 | bytes 3145728 | tf_op jit(solution)/shard_map/pallas_call | solution.py:237
  45.6 2.2 convolution_convert_fusion.6
  48.2 2.8 copy.75
  51.6 3.4 multiply_reduce_fusion.2
  55.1 2.0 fusion.128
  57.1 2.6 fusion.21
  61.2 2.5 fusion.22
  64.1 6.7 %multiply_convert_fusion = (bf16[4,320,1536]{2,1,0:T(8,128)(2,1)}, f32[4,320,1536]{2,1,0:T(8,128)}) fusion(bf16[4,320,768]{2,1,0:T(8,128)(2,1)S(1)} %bitcast.287, bf16[4,768,1536]{2,1,0:T(8,128)(2,1)S(1)} %bitcast.308), kind=kOutput, calls=%fused_computation.9 | convolution fusion | flops 3037593600 | bytes 23199744 | tf_op jit(solution)/shard_map/ecd,edf->ecf/dot_general | solution.py:401
  70.8 6.0 %convolution_convert_fusion.3 = bf16[2,768,1536]{2,1,0:T(8,128)(2,1)} fusion(bf16[2,320,768]{2,1,0:T(8,128)(2,1)S(1)} %bitcast.291, bf16[4,320,1536]{2,1,0:T(8,128)(2,1)} %get-tuple-element.20), kind=kOutput, calls=%fused_computation.30 | convolution fusion | flops 1512308736 | bytes 7667712 | tf_op jit(solution)/shard_map/ecd,ecf->edf/dot_general | solution.py:405
  76.8 4.8 %convolution_convert_fusion.2 = bf16[2,768,1536]{2,1,0:T(8,128)(2,1)} fusion(bf16[2,320,768]{2,1,0:T(8,128)(2,1)S(1)} %bitcast.290, bf16[4,320,1536]{2,1,0:T(8,128)(2,1)S(1)} %copy-done.52), kind=kOutput, calls=%fused_computation.29 | convolution fusion | flops 1512308736 | bytes 7667712 | tf_op jit(solution)/shard_map/ecd,ecf->edf/dot_general | solution.py:405
  81.6 14.4 %fusion.6 = bf16[4,320,1536]{2,1,0:T(8,128)(2,1)} fusion(f32[4,320,1536]{2,1,0:T(8,128)} %get-tuple-element.129, bf16[4,320,768]{2,1,0:T(8,128)(2,1)S(1)} %bitcast.286, bf16[4,1536,768]{2,1,0:T(8,128)(2,1)} %param.21), kind=kOutput, calls=%fused_computation.8 | convolution fusion | flops 3059220480 | bytes 23199744 | tf_op jit(solution)/shard_map/ecd,efd->ecf/dot_general | solution.py:410
  96.0 6.0 %convolution_convert_fusion.1 = bf16[2,768,1536]{2,1,0:T(8,128)(2,1)} fusion(bf16[2,320,768]{2,1,0:T(8,128)(2,1)S(1)} %bitcast.289, bf16[4,320,1536]{2,1,0:T(8,128)(2,1)} %fusion.6), kind=kOutput, calls=%fused_computation.28 | convolution fusion | flops 1512308736 | bytes 7667712 | tf_op jit(solution)/shard_map/ecd,ecf->edf/dot_general | solution.py:414
  102.0 6.1 %convolution_convert_fusion = bf16[2,768,1536]{2,1,0:T(8,128)(2,1)} fusion(bf16[2,320,768]{2,1,0:T(8,128)(2,1)S(1)} %bitcast.288, bf16[4,320,1536]{2,1,0:T(8,128)(2,1)} %fusion.6), kind=kOutput, calls=%fused_computation.27 | convolution fusion | flops 1512308736 | bytes 7667712 | tf_op jit(solution)/shard_map/ecd,ecf->edf/dot_general | solution.py:414
  108.2 3.2 convolution_convert_fusion.5
  111.4 2.5 fusion.53
  114.4 8.1 %convolution_convert_fusion.4 = bf16[4,320,768]{2,1,0:T(8,128)(2,1)S(1)} fusion(bf16[4,320,1536]{2,1,0:T(8,128)(2,1)} %fusion.6, bf16[4,768,1536]{2,1,0:T(8,128)(2,1)} %param.20), kind=kOutput, calls=%fused_computation.93 | convolution fusion | flops 3020881920 | bytes 15335424 | tf_op jit(solution)/shard_map/ecf,edf->ecd/dot_general | solution.py:421
  122.5 2.5 fusion.54
  125.3 1.9 constant_dynamic-slice_fusion.5
  128.9 2.5 collective-permute-start.20
  131.4 1.9 constant_dynamic-slice_fusion.7
  134.9 2.4 collective-permute-start.16
  137.3 1.9 constant_dynamic-slice_fusion.1
  140.9 1.9 constant_dynamic-slice_fusion.3
  144.4 2.7 fusion.36
  147.0 3.8 multiply_reduce_fusion
  150.9 4.6 convert_add_fusion
  156.5 1.8 convolution_convert_fusion.8
  158.3 2.6 copy.93
  162.6 40.2 %shard_map.205 = (bf16[3,1024,384]{2,1,0:T(8,128)(2,1)S(1)}, f32[3,2,768]{2,1,0:T(2,128)S(1)}) custom-call(s32[16]{0:T(128)S(1)} %pad_add_fusion.range_ref, bf16[3,1024,384]{2,1,0:T(8,128)(2,1)S(1)} %copy-done.7, bf16[3,1024,384]{2,1,0:T(8,128)(2,1)S(1)} %copy-done.7, bf16[3,1024,384]{2,1,0:T(8,128)(2,1)S(1)} %copy-done.7, ...), custom_call_target="tpu_custom_call" | custom-call | flops 19327352832 | bytes 6291456 | tf_op jit(solution)/shard_map/pallas_call | solution.py:257
  204.6 2.8 convolution_convert_fusion.9
  214.5 2.6 collective-permute-start.8
  217.1 3.4 bitcast_convert_fusion
  220.5 2.7 fusion.42
  223.2 23.2 %collective-permute-done.12 = bf16[2,2,2,2,48,384]{5,4,0,1,2,3:T(8,128)(2,1)} collective-permute-done((bf16[2,2,2,2,48,384]{5,4,0,1,2,3:T(8,128)(2,1)}, bf16[2,2,2,2,48,384]{5,4,0,1,2,3:T(8,128)(2,1)}, u32[]{:S(2)}, u32[]{:S(2)}) %collective-permute-start.12) | collective-permute-done | bytes 589856 | tf_op jit(solution)/shard_map/ppermute | solution.py:299
  246.5 2.5 collective-permute-start.24
  252.0 2.5 fusion.13
  257.4 2.5 fusion.14
  261.0 2.0 collective-permute-start.21
  263.1 2.6 fusion.11
  265.7 35.5 %collective-permute-done.24 = bf16[2,2,2,2,48,1536]{5,4,0,1,2,3:T(8,128)(2,1)S(1)} collective-permute-done((bf16[2,2,2,2,48,1536]{5,4,0,1,2,3:T(8,128)(2,1)}, bf16[2,2,2,2,48,1536]{5,4,0,1,2,3:T(8,128)(2,1)S(1)}, u32[]{:S(2)}, u32[]{:S(2)}) %collective-permute-start.24) | collective-permute-done | bytes 2359328 | tf_op jit(solution)/shard_map/ppermute | solution.py:299
  307.6 2.1 collective-permute-start.29
  309.7 1.9 collective-permute-start.14
  311.8 4.3 collective-permute-done.14
  316.1 2.1 collective-permute-start.10
  318.3 3.8 collective-permute-done.10
  322.1 2.2 collective-permute-start.15
  324.4 3.2 collective-permute-done.15
  327.6 2.0 collective-permute-start.11
  329.6 3.2 collective-permute-done.11
  337.0 20.5 %collective-permute-done.4 = f32[4800]{0:T(1024)S(1)} collective-permute-done((f32[4800]{0:T(1024)S(1)}, f32[4800]{0:T(1024)S(1)}, u32[]{:S(2)}, u32[]{:S(2)}) %collective-permute-start.4) | collective-permute-done | bytes 19232 | tf_op jit(solution)/shard_map/ppermute | solution.py:299
  361.4 1.8 collective-permute-start.6
  363.2 2.0 collective-permute-done.6
  365.1 2.7 collective-permute-start.7
  367.9 2.8 fusion.29
  370.7 3.5 copy.94
  376.2 2.1 fusion.47
  387.5 10.3 %collective-permute-done.22 = bf16[2,2,48,1536]{3,2,0,1:T(8,128)(2,1)S(1)} collective-permute-done((bf16[2,2,48,1536]{3,2,0,1:T(8,128)(2,1)S(1)}, bf16[2,2,48,1536]{3,2,0,1:T(8,128)(2,1)S(1)}, u32[]{:S(2)}, u32[]{:S(2)}) %collective-permute-start.22) | collective-permute-done | bytes 589856 | tf_op jit(solution)/shard_map/ppermute | solution.py:299
  398.1 18.7 %collective-permute-done.18 = bf16[2,2,48,1536]{3,2,0,1:T(8,128)(2,1)S(1)} collective-permute-done((bf16[2,2,48,1536]{3,2,0,1:T(8,128)(2,1)S(1)}, bf16[2,2,48,1536]{3,2,0,1:T(8,128)(2,1)S(1)}, u32[]{:S(2)}, u32[]{:S(2)}) %collective-permute-start.18) | collective-permute-done | bytes 589856 | tf_op jit(solution)/shard_map/ppermute | solution.py:299
  417.1 18.7 %collective-permute-done.30 = bf16[2,2,48,1536]{3,2,0,1:T(8,128)(2,1)S(1)} collective-permute-done((bf16[2,2,48,1536]{3,2,0,1:T(8,128)(2,1)S(1)}, bf16[2,2,48,1536]{3,2,0,1:T(8,128)(2,1)S(1)}, u32[]{:S(2)}, u32[]{:S(2)}) %collective-permute-start.30) | collective-permute-done | bytes 589856 | tf_op jit(solution)/shard_map/ppermute | solution.py:299
  436.0 7.4 %collective-permute-done.26 = bf16[2,2,48,1536]{3,2,0,1:T(8,128)(2,1)S(1)} collective-permute-done((bf16[2,2,48,1536]{3,2,0,1:T(8,128)(2,1)S(1)}, bf16[2,2,48,1536]{3,2,0,1:T(8,128)(2,1)S(1)}, u32[]{:S(2)}, u32[]{:S(2)}) %collective-permute-start.26) | collective-permute-done | bytes 589856 | tf_op jit(solution)/shard_map/ppermute | solution.py:299
  444.2 15.3 %collective-permute-done.31 = bf16[2,48,1536]{2,1,0:T(8,128)(2,1)S(1)} collective-permute-done((bf16[2,48,1536]{2,1,0:T(8,128)(2,1)S(1)}, bf16[2,48,1536]{2,1,0:T(8,128)(2,1)S(1)}, u32[]{:S(2)}, u32[]{:S(2)}) %collective-permute-start.31) | collective-permute-done | bytes 294944 | tf_op jit(solution)/shard_map/ppermute | solution.py:299
  460.7 2.0 collective-permute-done.27
  (323 shorter events, 74.6 us)
Async XLA Ops:
  0.6 18.3 %copy-start = (bf16[3,768,384]{2,1,0:T(8,128)(2,1)S(1)}, bf16[3,768,384]{2,1,0:T(8,128)(2,1)}, u32[]{:S(2)}) copy-start(bf16[3,768,384]{2,1,0:T(8,128)(2,1)} %param.15) | copy-start | bytes 5308420
  11.5 6.2 %copy-start.3 = (s32[1,1024]{1,0:T(1,128)S(1)}, s32[1,1024]{1,0:T(1,128)}, u32[]{:S(2)}) copy-start(s32[1,1024]{1,0:T(1,128)} %seg_row_ref.3) | copy-start | bytes 12292
  11.5 7.5 %copy-start.34 = (f32[768]{0:T(1024)S(1)}, f32[768]{0:T(1024)}, u32[]{:S(2)}) copy-start(f32[768]{0:T(1024)} %param.14) | copy-start | bytes 9220
  13.2 4.4 copy-start.12
  17.9 5.5 %copy-start.1 = (s32[1024,1]{1,0:T(8,128)}, s32[1024,1]{1,0:T(8,128)S(1)}, u32[]{:S(2)}) copy-start(s32[1024,1]{1,0:T(8,128)S(1)} %copy.74.seg_col_ref) | copy-start | bytes 12292
  19.0 3.9 copy-start.38
  19.0 3.9 copy-start.39
  19.0 3.9 copy-start.40
  19.0 3.9 copy-start.41
  22.9 22.7 %copy-start.6 = (bf16[3,1024,384]{2,1,0:T(8,128)(2,1)}, bf16[3,1024,384]{2,1,0:T(8,128)(2,1)S(1)}, u32[]{:S(2)}) copy-start(bf16[3,1024,384]{2,1,0:T(8,128)(2,1)S(1)} %convert_bitcast_fusion.1.q_ref.k_ref.v_ref) | copy-start | bytes 7077892
  23.4 22.2 %copy-start.29 = (bf16[384,768]{1,0:T(8,128)(2,1)S(1)}, bf16[384,768]{1,0:T(8,128)(2,1)}, u32[]{:S(2)}) copy-start(bf16[384,768]{1,0:T(8,128)(2,1)} %param.16) | copy-start | bytes 1769476
  47.8 3.8 collective-permute-start
  55.0 95.8 %copy-start.8 = (f32[1024,768]{0,1:T(8,128)}, f32[1024,768]{0,1:T(8,128)S(1)}, u32[]{:S(2)}) copy-start(f32[1024,768]{0,1:T(8,128)S(1)} %get-tuple-element.99) | copy-start | bytes 9437188
  59.8 4.1 slice-start.11
  70.8 6.0 %copy-start.52 = (bf16[4,320,1536]{2,1,0:T(8,128)(2,1)S(1)}, bf16[4,320,1536]{2,1,0:T(8,128)(2,1)}, u32[]{:S(2)}) copy-start(bf16[4,320,1536]{2,1,0:T(8,128)(2,1)} %get-tuple-element.20) | copy-start | bytes 11796484
  96.0 12.2 %slice-start.8 = ((s8[9437184]{0:T(1024)(128)(4,1)}), s8[4194304]{0:T(1024)(128)(4,1)S(1)}, s32[]{:S(2)}) async-start(s8[9437184]{0:T(1024)(128)(4,1)} %bitcast.305), calls=%async_computation.8 | async-start | bytes 8388608
  96.0 12.2 %slice-start.9 = ((s8[9437184]{0:T(1024)(128)(4,1)}), s8[4194304]{0:T(1024)(128)(4,1)S(1)}, s32[]{:S(2)}) async-start(s8[9437184]{0:T(1024)(128)(4,1)} %bitcast.305), calls=%async_computation.9 | async-start | bytes 8388608
  102.0 6.2 %slice-start.10 = ((s8[9437184]{0:T(1024)(128)(4,1)}), s8[1048576]{0:T(1024)(128)(4,1)S(1)}, s32[]{:S(2)}) async-start(s8[9437184]{0:T(1024)(128)(4,1)} %bitcast.305), calls=%async_computation.10 | async-start | bytes 2097152
  102.0 6.2 %copy-start.53 = (bf16[4,320,1536]{2,1,0:T(8,128)(2,1)S(1)}, bf16[4,320,1536]{2,1,0:T(8,128)(2,1)}, u32[]{:S(2)}) copy-start(bf16[4,320,1536]{2,1,0:T(8,128)(2,1)} %get-tuple-element.20) | copy-start | bytes 11796484
  114.0 30.4 %collective-permute-start.1 = (bf16[1024,768]{0,1:T(8,128)(2,1)S(1)}, bf16[1024,768]{0,1:T(8,128)(2,1)}, u32[]{:S(2)}, u32[]{:S(2)}) collective-permute-start(bf16[1024,768]{0,1:T(8,128)(2,1)S(1)} %fusion.53), channel_id=1, source_target_pairs={{0,1},{1,0},{2,3},{3,2},{4,5},{5,4},{6,7},{7,6},{8,9},{9,8},{10,11... | collective-permute-start | bytes 4718600 | tf_op jit(solution)/shard_map/ppermute | solution.py:288
  125.1 21.9 %collective-permute-start.2 = (bf16[1024,768]{0,1:T(8,128)(2,1)S(1)}, bf16[1024,768]{0,1:T(8,128)(2,1)S(1)}, u32[]{:S(2)}, u32[]{:S(2)}) collective-permute-start(bf16[1024,768]{0,1:T(8,128)(2,1)S(1)} %fusion.54), channel_id=1, source_target_pairs={{0,1},{1,0},{2,3},{3,2},{4,5},{5,4},{6,7},{7,6},{8,9},{9,8},{10,11... | collective-permute-start | bytes 4718600 | tf_op jit(solution)/shard_map/ppermute | solution.py:288
  125.3 6.1 %slice-start.4 = ((s8[4718592]{0:T(1024)(128)(4,1)}), s8[4194304]{0:T(1024)(128)(4,1)S(1)}, s32[]{:S(2)}) async-start(s8[4718592]{0:T(1024)(128)(4,1)} %bitcast.278), calls=%async_computation.4 | async-start | bytes 8388608
  125.3 6.1 %slice-start.5 = ((s8[4718592]{0:T(1024)(128)(4,1)}), s8[524288]{0:T(1024)(128)(4,1)S(1)}, s32[]{:S(2)}) async-start(s8[4718592]{0:T(1024)(128)(4,1)} %bitcast.278), calls=%async_computation.5 | async-start | bytes 1048576
  128.9 123.0 %collective-permute-start.20 = (bf16[2,2,2,2,48,1536]{5,4,0,1,2,3:T(8,128)(2,1)}, bf16[2,2,2,2,48,1536]{5,4,0,1,2,3:T(8,128)(2,1)}, u32[]{:S(2)}, u32[]{:S(2)}) collective-permute-start(bf16[2,2,2,2,48,1536]{5,4,0,1,2,3:T(8,128)(2,1)} %bitcast.264), channel_id=1, source_target_pairs={{0,4},{2,6},{4,0},{6,2},{8,12},{10,14},{12,8},{14,10},{16,20},{18,... | collective-permute-start | bytes 7077896 | tf_op jit(solution)/shard_map/ppermute | solution.py:299
  131.4 5.9 %slice-start.2 = ((s8[4718592]{0:T(1024)(128)(4,1)}), s8[4194304]{0:T(1024)(128)(4,1)S(1)}, s32[]{:S(2)}) async-start(s8[4718592]{0:T(1024)(128)(4,1)} %bitcast.275), calls=%async_computation.2 | async-start | bytes 8388608
  131.4 5.9 %slice-start.3 = ((s8[4718592]{0:T(1024)(128)(4,1)}), s8[524288]{0:T(1024)(128)(4,1)S(1)}, s32[]{:S(2)}) async-start(s8[4718592]{0:T(1024)(128)(4,1)} %bitcast.275), calls=%async_computation.3 | async-start | bytes 1048576
  134.9 120.7 %collective-permute-start.16 = (bf16[2,2,2,2,48,1536]{5,4,0,1,2,3:T(8,128)(2,1)}, bf16[2,2,2,2,48,1536]{5,4,0,1,2,3:T(8,128)(2,1)}, u32[]{:S(2)}, u32[]{:S(2)}) collective-permute-start(bf16[2,2,2,2,48,1536]{5,4,0,1,2,3:T(8,128)(2,1)} %bitcast.265), channel_id=1, source_target_pairs={{0,2},{2,0},{4,6},{6,4},{8,10},{10,8},{12,14},{14,12},{16,18},{18,... | collective-permute-start | bytes 7077896 | tf_op jit(solution)/shard_map/ppermute | solution.py:299
  140.9 120.1 %collective-permute-start.28 = (bf16[2,2,2,2,48,1536]{5,4,0,1,2,3:T(8,128)(2,1)}, bf16[2,2,2,2,48,1536]{5,4,0,1,2,3:T(8,128)(2,1)}, u32[]{:S(2)}, u32[]{:S(2)}) collective-permute-start(bf16[2,2,2,2,48,1536]{5,4,0,1,2,3:T(8,128)(2,1)} %bitcast.262), channel_id=1, source_target_pairs={{0,4},{2,6},{4,0},{6,2},{8,12},{10,14},{12,8},{14,10},{16,20},{18,... | collective-permute-start | bytes 7077896 | tf_op jit(solution)/shard_map/ppermute | solution.py:299
  150.9 4.6 copy-start.30
  204.6 5.9 %copy-start.13 = (bf16[1,1024,768]{1,2,0:T(8,128)(2,1)S(1)}, bf16[1,1024,768]{1,2,0:T(8,128)(2,1)}, u32[]{:S(2)}) copy-start(bf16[1,1024,768]{1,2,0:T(8,128)(2,1)} %copy-done.12) | copy-start | bytes 4718596
  209.2 37.2 %collective-permute-start.12 = (bf16[2,2,2,2,48,384]{5,4,0,1,2,3:T(8,128)(2,1)}, bf16[2,2,2,2,48,384]{5,4,0,1,2,3:T(8,128)(2,1)}, u32[]{:S(2)}, u32[]{:S(2)}) collective-permute-start(bf16[2,2,2,2,48,384]{5,4,0,1,2,3:T(8,128)(2,1)} %bitcast.266), channel_id=1, source_target_pairs={{0,4},{2,6},{4,0},{6,2},{8,12},{10,14},{12,8},{14,10},{16,20},{18,... | collective-permute-start | bytes 1769480 | tf_op jit(solution)/shard_map/ppermute | solution.py:299
  214.5 6.0 %copy-start.9 = (f32[1024,768]{0,1:T(8,128)S(1)}, f32[1024,768]{0,1:T(8,128)}, u32[]{:S(2)}) copy-start(f32[1024,768]{0,1:T(8,128)} %copy-done.8) | copy-start | bytes 9437188
  214.5 36.1 %collective-permute-start.8 = (bf16[2,2,2,2,48,384]{5,4,0,1,2,3:T(8,128)(2,1)}, bf16[2,2,2,2,48,384]{5,4,0,1,2,3:T(8,128)(2,1)}, u32[]{:S(2)}, u32[]{:S(2)}) collective-permute-start(bf16[2,2,2,2,48,384]{5,4,0,1,2,3:T(8,128)(2,1)} %bitcast.267), channel_id=1, source_target_pairs={{0,2},{2,0},{4,6},{6,4},{8,10},{10,8},{12,14},{14,12},{16,18},{18,... | collective-permute-start | bytes 1769480 | tf_op jit(solution)/shard_map/ppermute | solution.py:299
  223.2 27.3 %copy-start.26 = (bf16[1024,768]{0,1:T(8,128)(2,1)S(1)}, bf16[1024,768]{0,1:T(8,128)(2,1)}, u32[]{:S(2)}) copy-start(bf16[1024,768]{0,1:T(8,128)(2,1)} %bitcast_convert_fusion) | copy-start | bytes 4718596
  223.2 27.4 %copy-start.28 = (bf16[2,2,2,2,1,48,384]{6,5,4,3,2,1,0:T(8,128)(2,1)S(1)}, bf16[2,2,2,2,1,48,384]{6,5,4,3,2,1,0:T(8,128)(2,1)}, u32[]{:S(2)}) copy-start(bf16[2,2,2,2,1,48,384]{6,5,4,3,2,1,0:T(8,128)(2,1)} %get-tuple-element.114) | copy-start | bytes 1769476
  246.5 54.8 %collective-permute-start.24 = (bf16[2,2,2,2,48,1536]{5,4,0,1,2,3:T(8,128)(2,1)}, bf16[2,2,2,2,48,1536]{5,4,0,1,2,3:T(8,128)(2,1)S(1)}, u32[]{:S(2)}, u32[]{:S(2)}) collective-permute-start(bf16[2,2,2,2,48,1536]{5,4,0,1,2,3:T(8,128)(2,1)} %bitcast.285), channel_id=1, source_target_pairs={{0,2},{2,0},{4,6},{6,4},{8,10},{10,8},{12,14},{14,12},{16,18},{18,... | collective-permute-start | bytes 7077896 | tf_op jit(solution)/shard_map/ppermute | solution.py:299
  250.5 84.0 %collective-permute-start.3 = (bf16[1024,768]{0,1:T(8,128)(2,1)S(1)}, bf16[1024,768]{0,1:T(8,128)(2,1)S(1)}, u32[]{:S(2)}, u32[]{:S(2)}) collective-permute-start(bf16[1024,768]{0,1:T(8,128)(2,1)S(1)} %copy-done.26), channel_id=1, source_target_pairs={{0,1},{1,0},{2,3},{3,2},{4,5},{5,4},{6,7},{7,6},{8,9},{9,8},{10,11... | collective-permute-start | bytes 4718600 | tf_op jit(solution)/shard_map/ppermute | solution.py:288
  251.9 55.7 %collective-permute-start.13 = (bf16[2,2,2,48,384]{4,3,0,1,2:T(8,128)(2,1)S(1)}, bf16[2,2,2,48,384]{4,3,0,1,2:T(8,128)(2,1)S(1)}, u32[]{:S(2)}, u32[]{:S(2)}) collective-permute-start(bf16[2,2,2,48,384]{4,3,0,1,2:T(8,128)(2,1)S(1)} %dynamic-slice_bitcast_fusion.12), channel_id=1, source_target_pairs={{0,2},{2,0},{4,6},{6,4},{8,10},{10,8},{12,14},{14,12},{16,18},{18,... | collective-permute-start | bytes 884744 | tf_op jit(solution)/shard_map/ppermute | solution.py:299
  255.6 54.1 %collective-permute-start.9 = (bf16[2,2,2,48,384]{4,3,0,1,2:T(8,128)(2,1)S(1)}, bf16[2,2,2,48,384]{4,3,0,1,2:T(8,128)(2,1)S(1)}, u32[]{:S(2)}, u32[]{:S(2)}) collective-permute-start(bf16[2,2,2,48,384]{4,3,0,1,2:T(8,128)(2,1)S(1)} %dynamic-slice_bitcast_fusion.13), channel_id=1, source_target_pairs={{0,4},{2,6},{4,0},{6,2},{8,12},{10,14},{12,8},{14,10},{16,20},{18,... | collective-permute-start | bytes 884744 | tf_op jit(solution)/shard_map/ppermute | solution.py:299
  259.9 5.8 %copy-start.22 = (bf16[2,2,2,2,48,1536]{5,4,0,1,2,3:T(8,128)(2,1)}, bf16[2,2,2,2,48,1536]{5,4,0,1,2,3:T(8,128)(2,1)S(1)}, u32[]{:S(2)}) copy-start(bf16[2,2,2,2,48,1536]{5,4,0,1,2,3:T(8,128)(2,1)S(1)} %fusion.14) | copy-start | bytes 7077892
  261.0 115.1 %collective-permute-start.21 = (bf16[2,2,2,48,1536]{4,3,0,1,2:T(8,128)(2,1)}, bf16[2,2,2,48,1536]{4,3,0,1,2:T(8,128)(2,1)}, u32[]{:S(2)}, u32[]{:S(2)}) collective-permute-start(bf16[2,2,2,48,1536]{4,3,0,1,2:T(8,128)(2,1)} %dynamic-slice_bitcast_fusion.2), channel_id=1, source_target_pairs={{0,2},{2,0},{4,6},{6,4},{8,10},{10,8},{12,14},{14,12},{16,18},{18,... | collective-permute-start | bytes 3538952 | tf_op jit(solution)/shard_map/ppermute | solution.py:299
  263.1 40.0 %copy-start.15 = (bf16[2,2,2,2,1,48,1536]{6,5,4,3,2,1,0:T(8,128)(2,1)S(1)}, bf16[2,2,2,2,1,48,1536]{6,5,4,3,2,1,0:T(8,128)(2,1)}, u32[]{:S(2)}) copy-start(bf16[2,2,2,2,1,48,1536]{6,5,4,3,2,1,0:T(8,128)(2,1)} %get-tuple-element.100) | copy-start | bytes 7077892
  265.7 38.1 %copy-start.24 = (bf16[2,2,2,2,48,1536]{5,4,0,1,2,3:T(8,128)(2,1)}, bf16[2,2,2,2,48,1536]{5,4,0,1,2,3:T(8,128)(2,1)S(1)}, u32[]{:S(2)}) copy-start(bf16[2,2,2,2,48,1536]{5,4,0,1,2,3:T(8,128)(2,1)S(1)} %fusion.11) | copy-start | bytes 7077892
  301.2 78.5 %collective-permute-start.17 = (bf16[2,2,2,48,1536]{4,3,0,1,2:T(8,128)(2,1)}, bf16[2,2,2,48,1536]{4,3,0,1,2:T(8,128)(2,1)}, u32[]{:S(2)}, u32[]{:S(2)}) collective-permute-start(bf16[2,2,2,48,1536]{4,3,0,1,2:T(8,128)(2,1)} %dynamic-slice_bitcast_fusion.3), channel_id=1, source_target_pairs={{0,4},{2,6},{4,0},{6,2},{8,12},{10,14},{12,8},{14,10},{16,20},{18,... | collective-permute-start | bytes 3538952 | tf_op jit(solution)/shard_map/ppermute | solution.py:299
  307.6 74.6 %collective-permute-start.29 = (bf16[2,2,2,48,1536]{4,3,0,1,2:T(8,128)(2,1)}, bf16[2,2,2,48,1536]{4,3,0,1,2:T(8,128)(2,1)}, u32[]{:S(2)}, u32[]{:S(2)}) collective-permute-start(bf16[2,2,2,48,1536]{4,3,0,1,2:T(8,128)(2,1)} %dynamic-slice_bitcast_fusion), channel_id=1, source_target_pairs={{0,2},{2,0},{4,6},{6,4},{8,10},{10,8},{12,14},{14,12},{16,18},{18,... | collective-permute-start | bytes 3538952 | tf_op jit(solution)/shard_map/ppermute | solution.py:299
  309.7 6.4 %collective-permute-start.14 = (bf16[2,2,48,384]{3,2,0,1:T(8,128)(2,1)S(1)}, bf16[2,2,48,384]{3,2,0,1:T(8,128)(2,1)S(1)}, u32[]{:S(2)}, u32[]{:S(2)}) collective-permute-start(bf16[2,2,48,384]{3,2,0,1:T(8,128)(2,1)S(1)} %dynamic-slice_bitcast_fusion.14), channel_id=1, source_target_pairs={{0,8},{2,10},{4,12},{6,14},{8,0},{10,2},{12,4},{14,6},{16,24},{18,... | collective-permute-start | bytes 442376 | tf_op jit(solution)/shard_map/ppermute | solution.py:299
  316.1 6.0 %collective-permute-start.10 = (bf16[2,2,48,384]{3,2,0,1:T(8,128)(2,1)S(1)}, bf16[2,2,48,384]{3,2,0,1:T(8,128)(2,1)S(1)}, u32[]{:S(2)}, u32[]{:S(2)}) collective-permute-start(bf16[2,2,48,384]{3,2,0,1:T(8,128)(2,1)S(1)} %dynamic-slice_bitcast_fusion.15), channel_id=1, source_target_pairs={{0,8},{2,10},{4,12},{6,14},{8,0},{10,2},{12,4},{14,6},{16,24},{18,... | collective-permute-start | bytes 442376 | tf_op jit(solution)/shard_map/ppermute | solution.py:299
  322.1 5.5 %collective-permute-start.15 = (bf16[2,48,384]{2,1,0:T(8,128)(2,1)S(1)}, bf16[2,48,384]{2,1,0:T(8,128)(2,1)S(1)}, u32[]{:S(2)}, u32[]{:S(2)}) collective-permute-start(bf16[2,48,384]{2,1,0:T(8,128)(2,1)S(1)} %dynamic-slice_bitcast_fusion.16), channel_id=1, source_target_pairs={{0,16},{2,18},{4,20},{6,22},{8,24},{10,26},{12,28},{14,30},{16,0},... | collective-permute-start | bytes 221192 | tf_op jit(solution)/shard_map/ppermute | solution.py:299
  327.6 5.3 %collective-permute-start.11 = (bf16[2,48,384]{2,1,0:T(8,128)(2,1)S(1)}, bf16[2,48,384]{2,1,0:T(8,128)(2,1)S(1)}, u32[]{:S(2)}, u32[]{:S(2)}) collective-permute-start(bf16[2,48,384]{2,1,0:T(8,128)(2,1)S(1)} %dynamic-slice_bitcast_fusion.17), channel_id=1, source_target_pairs={{0,16},{2,18},{4,20},{6,22},{8,24},{10,26},{12,28},{14,30},{16,0},... | collective-permute-start | bytes 221192 | tf_op jit(solution)/shard_map/ppermute | solution.py:299
  332.8 52.3 %collective-permute-start.25 = (bf16[2,2,2,48,1536]{4,3,0,1,2:T(8,128)(2,1)}, bf16[2,2,2,48,1536]{4,3,0,1,2:T(8,128)(2,1)}, u32[]{:S(2)}, u32[]{:S(2)}) collective-permute-start(bf16[2,2,2,48,1536]{4,3,0,1,2:T(8,128)(2,1)} %dynamic-slice_bitcast_fusion.1), channel_id=1, source_target_pairs={{0,4},{2,6},{4,0},{6,2},{8,12},{10,14},{12,8},{14,10},{16,20},{18,... | collective-permute-start | bytes 3538952 | tf_op jit(solution)/shard_map/ppermute | solution.py:299
  334.6 33.3 %copy-start.11 = (f32[1024,768]{0,1:T(8,128)S(1)}, f32[1024,768]{0,1:T(8,128)}, u32[]{:S(2)}) copy-start(f32[1024,768]{0,1:T(8,128)} %copy-done.10) | copy-start | bytes 9437188
  334.6 33.3 %copy-start.35 = (f32[1024]{0:T(1024)S(1)}, f32[1024]{0:T(1024)}, u32[]{:S(2)}) copy-start(f32[1024]{0:T(1024)} %get-tuple-element.120) | copy-start | bytes 12292
  336.2 21.3 %collective-permute-start.4 = (f32[4800]{0:T(1024)S(1)}, f32[4800]{0:T(1024)S(1)}, u32[]{:S(2)}, u32[]{:S(2)}) collective-permute-start(f32[4800]{0:T(1024)S(1)} %pad_maximum_fusion.2), channel_id=1, source_target_pairs={{0,2},{2,0},{4,6},{6,4},{8,10},{10,8},{12,14},{14,12},{16,18},{18,... | collective-permute-start | bytes 57608 | tf_op jit(solution)/shard_map/ppermute | solution.py:299
  357.5 3.8 collective-permute-start.5
  361.4 3.8 collective-permute-start.6
  365.1 9.1 %collective-permute-start.7 = (f32[4800]{0:T(1024)S(1)}, f32[4800]{0:T(1024)S(1)}, u32[]{:S(2)}, u32[]{:S(2)}) collective-permute-start(f32[4800]{0:T(1024)S(1)} %add.1659), channel_id=1, source_target_pairs={{0,16},{2,18},{4,20},{6,22},{8,24},{10,26},{12,28},{14,30},{16,0},... | collective-permute-start | bytes 57608 | tf_op jit(solution)/shard_map/ppermute | solution.py:299
  378.3 19.5 %collective-permute-start.22 = (bf16[2,2,48,1536]{3,2,0,1:T(8,128)(2,1)S(1)}, bf16[2,2,48,1536]{3,2,0,1:T(8,128)(2,1)S(1)}, u32[]{:S(2)}, u32[]{:S(2)}) collective-permute-start(bf16[2,2,48,1536]{3,2,0,1:T(8,128)(2,1)S(1)} %dynamic-slice_bitcast_fusion.6), channel_id=1, source_target_pairs={{0,8},{2,10},{4,12},{6,14},{8,0},{10,2},{12,4},{14,6},{16,24},{18,... | collective-permute-start | bytes 1769480 | tf_op jit(solution)/shard_map/ppermute | solution.py:299
  381.4 35.4 %collective-permute-start.18 = (bf16[2,2,48,1536]{3,2,0,1:T(8,128)(2,1)S(1)}, bf16[2,2,48,1536]{3,2,0,1:T(8,128)(2,1)S(1)}, u32[]{:S(2)}, u32[]{:S(2)}) collective-permute-start(bf16[2,2,48,1536]{3,2,0,1:T(8,128)(2,1)S(1)} %dynamic-slice_bitcast_fusion.7), channel_id=1, source_target_pairs={{0,8},{2,10},{4,12},{6,14},{8,0},{10,2},{12,4},{14,6},{16,24},{18,... | collective-permute-start | bytes 1769480 | tf_op jit(solution)/shard_map/ppermute | solution.py:299
  383.7 52.0 %collective-permute-start.30 = (bf16[2,2,48,1536]{3,2,0,1:T(8,128)(2,1)S(1)}, bf16[2,2,48,1536]{3,2,0,1:T(8,128)(2,1)S(1)}, u32[]{:S(2)}, u32[]{:S(2)}) collective-permute-start(bf16[2,2,48,1536]{3,2,0,1:T(8,128)(2,1)S(1)} %dynamic-slice_bitcast_fusion.4), channel_id=1, source_target_pairs={{0,8},{2,10},{4,12},{6,14},{8,0},{10,2},{12,4},{14,6},{16,24},{18,... | collective-permute-start | bytes 1769480 | tf_op jit(solution)/shard_map/ppermute | solution.py:299
  386.7 56.7 %collective-permute-start.26 = (bf16[2,2,48,1536]{3,2,0,1:T(8,128)(2,1)S(1)}, bf16[2,2,48,1536]{3,2,0,1:T(8,128)(2,1)S(1)}, u32[]{:S(2)}, u32[]{:S(2)}) collective-permute-start(bf16[2,2,48,1536]{3,2,0,1:T(8,128)(2,1)S(1)} %dynamic-slice_bitcast_fusion.5), channel_id=1, source_target_pairs={{0,8},{2,10},{4,12},{6,14},{8,0},{10,2},{12,4},{14,6},{16,24},{18,... | collective-permute-start | bytes 1769480 | tf_op jit(solution)/shard_map/ppermute | solution.py:299
  398.0 45.6 %collective-permute-start.23 = (bf16[2,48,1536]{2,1,0:T(8,128)(2,1)S(1)}, bf16[2,48,1536]{2,1,0:T(8,128)(2,1)S(1)}, u32[]{:S(2)}, u32[]{:S(2)}) collective-permute-start(bf16[2,48,1536]{2,1,0:T(8,128)(2,1)S(1)} %dynamic-slice_bitcast_fusion.10), channel_id=1, source_target_pairs={{0,16},{2,18},{4,20},{6,22},{8,24},{10,26},{12,28},{14,30},{16,0},... | collective-permute-start | bytes 884744 | tf_op jit(solution)/shard_map/ppermute | solution.py:299
  417.0 27.1 %collective-permute-start.19 = (bf16[2,48,1536]{2,1,0:T(8,128)(2,1)S(1)}, bf16[2,48,1536]{2,1,0:T(8,128)(2,1)S(1)}, u32[]{:S(2)}, u32[]{:S(2)}) collective-permute-start(bf16[2,48,1536]{2,1,0:T(8,128)(2,1)S(1)} %dynamic-slice_bitcast_fusion.11), channel_id=1, source_target_pairs={{0,16},{2,18},{4,20},{6,22},{8,24},{10,26},{12,28},{14,30},{16,0},... | collective-permute-start | bytes 884744 | tf_op jit(solution)/shard_map/ppermute | solution.py:299
  435.9 23.5 %collective-permute-start.31 = (bf16[2,48,1536]{2,1,0:T(8,128)(2,1)S(1)}, bf16[2,48,1536]{2,1,0:T(8,128)(2,1)S(1)}, u32[]{:S(2)}, u32[]{:S(2)}) collective-permute-start(bf16[2,48,1536]{2,1,0:T(8,128)(2,1)S(1)} %dynamic-slice_bitcast_fusion.8), channel_id=1, source_target_pairs={{0,16},{2,18},{4,20},{6,22},{8,24},{10,26},{12,28},{14,30},{16,0},... | collective-permute-start | bytes 884744 | tf_op jit(solution)/shard_map/ppermute | solution.py:299
  443.6 19.1 %collective-permute-start.27 = (bf16[2,48,1536]{2,1,0:T(8,128)(2,1)S(1)}, bf16[2,48,1536]{2,1,0:T(8,128)(2,1)S(1)}, u32[]{:S(2)}, u32[]{:S(2)}) collective-permute-start(bf16[2,48,1536]{2,1,0:T(8,128)(2,1)S(1)} %dynamic-slice_bitcast_fusion.9), channel_id=1, source_target_pairs={{0,16},{2,18},{4,20},{6,22},{8,24},{10,26},{12,28},{14,30},{16,0},... | collective-permute-start | bytes 884744 | tf_op jit(solution)/shard_map/ppermute | solution.py:299
  (36 other events, 117.2 us)
